TPU v7x, 128 devices: a whole 4x4x4 slice. The times are simulated.
128 devices in a mesh: section: 2 (over core), seq: 4 (over y), fsdp: 16 (over x, z).
Axes of the slice: x: 4, y: 4, z: 4, core: 2. Of those that a mesh axis runs over, the one named last changes fastest.
Arguments:
- tokens_in: bfloat16 [2, 16, 256, 768], P(None, 'fsdp', 'seq'), may hold values from -6 to 6
- cotangent: bfloat16 [2, 16, 256, 768], P(None, 'fsdp', 'seq'), may hold values from -6 to 6
- positions: int32 [2, 16, 256], P(None, 'fsdp', 'seq'), may hold values from 0 to 511, as said below
- first_gain: bfloat16 [2, 768], P('section', 'fsdp'), may hold values from 0.5 to 1.5
- first_bias: bfloat16 [2, 768], P('section', 'fsdp'), may hold values from -1.5 to 1.5
- second_gain: bfloat16 [2, 768], P('section', 'fsdp'), may hold values from 0.5 to 1.5
- second_bias: bfloat16 [2, 768], P('section', 'fsdp'), may hold values from -1.5 to 1.5
- qkv_weight: bfloat16 [2, 768, 2304], P('section', 'fsdp'), may hold values from -0.21875 to 0.21875
- qkv_bias: bfloat16 [2, 2304], P('section', 'fsdp'), may hold values from -1.5 to 1.5
- dense_weight: bfloat16 [2, 768, 768], P('section', 'fsdp'), may hold values from -1.75 to 1.75
- dense_bias: bfloat16 [2, 768], P('section', 'fsdp'), may hold values from -1.5 to 1.5
- expand_weight: bfloat16 [2, 768, 3072], P('section', 'fsdp'), may hold values from -0.21875 to 0.21875
- expand_bias: bfloat16 [2, 3072], P('section', 'fsdp'), may hold values from -1.5 to 1.5
- shrink_weight: bfloat16 [2, 3072, 768], P('section', 'fsdp'), may hold values from -0.15625 to 0.15625
- shrink_bias: bfloat16 [2, 768], P('section', 'fsdp'), may hold values from -1.5 to 1.5
Outputs:
- layer_out: bfloat16 [2, 2, 16, 256, 768], P('section', None, 'fsdp', 'seq')
- input_grad: bfloat16 [2, 2, 16, 256, 768], P('section', None, 'fsdp', 'seq')
- first_gain_grad: float32 [2, 768], P('section', 'fsdp')
- first_bias_grad: float32 [2, 768], P('section', 'fsdp')
- second_gain_grad: float32 [2, 768], P('section', 'fsdp')
- second_bias_grad: float32 [2, 768], P('section', 'fsdp')
- qkv_weight_grad: float32 [2, 768, 2304], P('section', 'fsdp')
- qkv_bias_grad: float32 [2, 2304], P('section', 'fsdp')
- dense_weight_grad: float32 [2, 768, 768], P('section', 'fsdp')
- dense_bias_grad: float32 [2, 768], P('section', 'fsdp')
- expand_weight_grad: float32 [2, 768, 3072], P('section', 'fsdp')
- expand_bias_grad: float32 [2, 3072], P('section', 'fsdp')
- shrink_weight_grad: float32 [2, 3072, 768], P('section', 'fsdp')
- shrink_bias_grad: float32 [2, 768], P('section', 'fsdp')
Inputs may be any that keep to these rules, and one draw needn't show every extreme that they name: `positions`: in every sequence the position of token i is 2 i or 2 i + 1.
All inputs are finite; a program needn't handle non-finite values.
Results may differ from a plain program's by a relative error of at most 0.02.
Values may be sent and summed in bfloat16 or wider, within the bound.
A program may use at most 128 MiB of HBM per device.

v0:
```python
from functools import partial
import math

import jax
import jax.numpy as jnp
from jax import lax
from jax.sharding import PartitionSpec as P

HD = 64
ROT = 16


def shifted(array, axis, by):
    size = lax.axis_size(axis)
    pairs = [(i, i + by) for i in range(size) if 0 <= i + by < size]
    return lax.ppermute(array, axis, pairs)


def layer_norm(values, scaling, offset_vec):
    center = values - jnp.mean(values, axis=-1, keepdims=True)
    spread = jnp.mean(center * center, axis=-1, keepdims=True)
    return center * lax.rsqrt(spread + 1e-05) * scaling + offset_vec


def rotary_tables(places, rot_width):
    half_width = rot_width // 2
    exponent = jnp.arange(half_width, dtype=jnp.float32) * (2.0 / rot_width)
    frequency = jnp.exp(-math.log(10000.0) * exponent)
    angles = places.astype(jnp.float32)[..., None] * frequency
    angles = jnp.concatenate([angles, angles], axis=-1)
    return (jnp.cos(angles), jnp.sin(angles))


def rotate(head_vals, cosine, sine, rot_width):
    rotated_part = head_vals[..., :rot_width]
    half_width = rot_width // 2
    turned = jnp.concatenate(
        [-rotated_part[..., half_width:], rotated_part[..., :half_width]], axis=-1
    )
    rotated = rotated_part * cosine + turned * sine
    return jnp.concatenate([rotated, head_vals[..., rot_width:]], axis=-1)


def matmul_f32(left_side, right_side):
    return jnp.dot(left_side, right_side, preferred_element_type=jnp.float32)


def contract_rows(left_side, right_side):
    return lax.dot_general(
        left_side, right_side, (((0,), (0,)), ((), ())), preferred_element_type=jnp.float32
    )


def contract_cols(left_side, right_side):
    return lax.dot_general(
        left_side, right_side, (((1,), (1,)), ((), ())), preferred_element_type=jnp.float32
    )


def split_heads(joined_heads):
    length = joined_heads.shape[0]
    head_count = joined_heads.shape[2] // HD
    queries = joined_heads[:, 0].reshape(length, head_count, HD)
    key_heads = joined_heads[:, 1].reshape(length, head_count, HD)
    value_heads = joined_heads[:, 2].reshape(length, head_count, HD)
    return (queries, key_heads, value_heads)


def block_scores(query_block, key_heads, block_rows, length):
    scores = jnp.einsum(
        "qhd,khd->hqk", query_block, key_heads, preferred_element_type=jnp.float32
    ) * HD ** (-0.5)
    row_index = jnp.arange(block_rows)
    allowed = row_index[:, None] >= jnp.arange(length)[None, :]
    return jnp.where(allowed[None], scores, -1e30)


def attend_forward(joined_heads):
    length = joined_heads.shape[0]
    local_width = joined_heads.shape[2]
    queries, key_heads, value_heads = split_heads(joined_heads)
    block_rows = min(512, length)
    scores = block_scores(queries, key_heads, block_rows, length)
    row_max = jnp.max(scores, axis=-1, keepdims=True)
    powers = jnp.exp(scores - row_max)
    row_total = jnp.sum(powers, axis=-1, keepdims=True)
    attn_probs = (powers / row_total).astype(jnp.bfloat16)
    context = jnp.einsum(
        "hqk,khd->qhd", attn_probs, value_heads, preferred_element_type=jnp.float32
    )
    outputs = context.astype(jnp.bfloat16).reshape(block_rows, local_width)
    totals = (row_max + jnp.log(row_total))[..., 0]
    return (outputs, totals)


def attend_backward(joined_heads, context_grad, totals):
    length = joined_heads.shape[0]
    local_width = joined_heads.shape[2]
    queries, key_heads, value_heads = split_heads(joined_heads)
    head_count = local_width // HD
    upstream = context_grad.reshape(length, head_count, HD)
    score_scale = HD ** (-0.5)
    block_rows = min(512, length)
    scores = block_scores(queries, key_heads, block_rows, length)
    attn_probs = jnp.exp(scores - totals[:, 0:block_rows, None])
    prob_grad = jnp.einsum(
        "qhd,khd->hqk", upstream, value_heads, preferred_element_type=jnp.float32
    )
    inner_sum = jnp.sum(attn_probs * prob_grad, axis=-1, keepdims=True)
    score_grad = (attn_probs * (prob_grad - inner_sum)).astype(jnp.bfloat16)
    query_part = (
        jnp.einsum("hqk,khd->qhd", score_grad, key_heads, preferred_element_type=jnp.float32)
        * score_scale
    )
    query_grads = query_part.astype(jnp.bfloat16).reshape(block_rows, local_width)
    key_grad = (
        jnp.einsum("hqk,qhd->khd", score_grad, queries, preferred_element_type=jnp.float32)
        * score_scale
    )
    value_grad = jnp.einsum(
        "hqk,qhd->khd",
        attn_probs.astype(jnp.bfloat16),
        upstream,
        preferred_element_type=jnp.float32,
    )
    return jnp.stack(
        [
            query_grads,
            key_grad.astype(jnp.bfloat16).reshape(length, local_width),
            value_grad.astype(jnp.bfloat16).reshape(length, local_width),
        ],
        axis=1,
    )


def layer_forward(layer_in, places, weights):
    (
        first_gain,
        first_bias,
        second_gain,
        second_bias,
        qkv_weight,
        qkv_bias,
        dense_weight,
        dense_bias,
        expand_weight,
        expand_bias,
        shrink_weight,
        shrink_bias,
    ) = weights
    tok_count, width = layer_in.shape
    head_total = width // HD
    first = layer_norm(
        layer_in, first_gain.astype(jnp.float32), first_bias.astype(jnp.float32)
    ).astype(jnp.bfloat16)
    joined = (matmul_f32(first, qkv_weight) + qkv_bias.astype(jnp.float32)).reshape(
        tok_count, 3, head_total, HD
    )
    cosine, sine = rotary_tables(places, ROT)
    cosine = cosine[:, None, :]
    sine = sine[:, None, :]
    queries = rotate(joined[:, 0], cosine, sine, ROT).astype(jnp.bfloat16).reshape(tok_count, width)
    key_rows = (
        rotate(joined[:, 1], cosine, sine, ROT).astype(jnp.bfloat16).reshape(tok_count, width)
    )
    value_rows = joined[:, 2].astype(jnp.bfloat16).reshape(tok_count, width)
    stacked = jnp.stack([queries, key_rows, value_rows], axis=1)
    gathered_heads = lax.all_to_all(stacked, "seq", split_axis=2, concat_axis=0, tiled=True)
    context_heads, totals = attend_forward(gathered_heads)
    context = lax.all_to_all(context_heads, "seq", split_axis=0, concat_axis=1, tiled=True)
    attended = matmul_f32(context, dense_weight) + dense_bias.astype(jnp.float32)
    second = layer_norm(
        layer_in, second_gain.astype(jnp.float32), second_bias.astype(jnp.float32)
    ).astype(jnp.bfloat16)
    hidden = matmul_f32(second, expand_weight) + expand_bias.astype(jnp.float32)
    active = jax.nn.gelu(hidden, approximate=False).astype(jnp.bfloat16)
    result = (
        layer_in + attended + matmul_f32(active, shrink_weight) + shrink_bias.astype(jnp.float32)
    )
    return (result, (gathered_heads, totals, context, hidden))


def layer_backward(layer_in, places, weights, kept_state, out_grad):
    (
        first_gain,
        first_bias,
        second_gain,
        second_bias,
        qkv_weight,
        qkv_bias,
        dense_weight,
        dense_bias,
        expand_weight,
        expand_bias,
        shrink_weight,
        shrink_bias,
    ) = weights
    gathered_heads, totals, context, hidden = kept_state
    tok_count, width = layer_in.shape
    head_total = width // HD
    grad_full = out_grad.astype(jnp.float32)
    first_value, first_pull = jax.vjp(
        layer_norm, layer_in, first_gain.astype(jnp.float32), first_bias.astype(jnp.float32)
    )
    second_value, second_pull = jax.vjp(
        layer_norm, layer_in, second_gain.astype(jnp.float32), second_bias.astype(jnp.float32)
    )
    first = first_value.astype(jnp.bfloat16)
    second = second_value.astype(jnp.bfloat16)
    active_value, gelu_pull = jax.vjp(partial(jax.nn.gelu, approximate=False), hidden)
    active = active_value.astype(jnp.bfloat16)
    shrink_grad = contract_rows(active, out_grad)
    shrink_bias_grad = jnp.sum(grad_full, axis=0)
    hidden_grad = gelu_pull(contract_cols(out_grad, shrink_weight))[0].astype(jnp.bfloat16)
    expand_grad = contract_rows(second, hidden_grad)
    expand_bias_grad = jnp.sum(hidden_grad.astype(jnp.float32), axis=0)
    second_norm_grad = contract_cols(hidden_grad, expand_weight)
    dense_grad = contract_rows(context, out_grad)
    dense_bias_grad = jnp.sum(grad_full, axis=0)
    context_grad = contract_cols(out_grad, dense_weight).astype(jnp.bfloat16)
    context_heads_grad = lax.all_to_all(
        context_grad, "seq", split_axis=1, concat_axis=0, tiled=True
    )
    joined_heads_grad = attend_backward(gathered_heads, context_heads_grad, totals)
    joined_grad = lax.all_to_all(joined_heads_grad, "seq", split_axis=0, concat_axis=2, tiled=True)
    cosine, sine = rotary_tables(places, ROT)
    cosine = cosine[:, None, :]
    sine = sine[:, None, :]
    query_back = rotate(
        joined_grad[:, 0].astype(jnp.float32).reshape(tok_count, head_total, HD), cosine, -sine, ROT
    )
    key_back = rotate(
        joined_grad[:, 1].astype(jnp.float32).reshape(tok_count, head_total, HD), cosine, -sine, ROT
    )
    joined_flat = jnp.stack(
        [
            query_back.astype(jnp.bfloat16).reshape(tok_count, width),
            key_back.astype(jnp.bfloat16).reshape(tok_count, width),
            joined_grad[:, 2],
        ],
        axis=1,
    ).reshape(tok_count, 3 * width)
    qkv_grad = contract_rows(first, joined_flat)
    qkv_bias_grad = jnp.sum(joined_flat.astype(jnp.float32), axis=0)
    first_norm_grad = contract_cols(joined_flat, qkv_weight)
    first_in_grad, first_gain_grad, first_bias_grad = first_pull(first_norm_grad)
    second_in_grad, second_gain_grad, second_bias_grad = second_pull(second_norm_grad)
    input_grad = grad_full + first_in_grad + second_in_grad
    layer_grads = (
        first_gain_grad,
        first_bias_grad,
        second_gain_grad,
        second_bias_grad,
        qkv_grad,
        qkv_bias_grad,
        dense_grad,
        dense_bias_grad,
        expand_grad,
        expand_bias_grad,
        shrink_grad,
        shrink_bias_grad,
    )
    return (input_grad, layer_grads)


def stack_all(*members):
    return jnp.stack(members)


def pick_slot(tick_slot, stacked):
    return lax.dynamic_index_in_dim(stacked, tick_slot, 0, keepdims=False)


def on_device(
    tokens_in,
    cotangent,
    positions,
    first_gain,
    first_bias,
    second_gain,
    second_bias,
    qkv_weight,
    qkv_bias,
    dense_weight,
    dense_bias,
    expand_weight,
    expand_bias,
    shrink_weight,
    shrink_bias,
):
    section_index = lax.axis_index("section")
    micro_count = tokens_in.shape[0]
    tok_count = tokens_in.shape[2]
    width = tokens_in.shape[3]
    gathered = (
        lax.all_gather(first_gain, "fsdp", axis=1, tiled=True),
        lax.all_gather(first_bias, "fsdp", axis=1, tiled=True),
        lax.all_gather(second_gain, "fsdp", axis=1, tiled=True),
        lax.all_gather(second_bias, "fsdp", axis=1, tiled=True),
        lax.all_gather(qkv_weight, "fsdp", axis=1, tiled=True),
        lax.all_gather(qkv_bias, "fsdp", axis=1, tiled=True),
        lax.all_gather(dense_weight, "fsdp", axis=1, tiled=True),
        lax.all_gather(dense_bias, "fsdp", axis=1, tiled=True),
        lax.all_gather(expand_weight, "fsdp", axis=1, tiled=True),
        lax.all_gather(expand_bias, "fsdp", axis=1, tiled=True),
        lax.all_gather(shrink_weight, "fsdp", axis=1, tiled=True),
        lax.all_gather(shrink_bias, "fsdp", axis=1, tiled=True),
    )
    weights = tuple((member[0] for member in gathered))
    own_inputs = tokens_in[:, 0]
    own_seeds = cotangent[:, 0]
    own_places = positions[:, 0]
    is_first = section_index == 0
    arrived = jnp.zeros((tok_count, width), jnp.bfloat16)
    results = []
    kept_list = []
    inputs_list = []
    for moment in range(micro_count + 1):
        index_here = jnp.clip(moment - section_index, 0, micro_count - 1)
        places = lax.dynamic_index_in_dim(own_places, index_here, 0, keepdims=False)
        layer_low = jnp.where(is_first, own_inputs[min(moment, micro_count - 1)], arrived)
        result, kept_state = layer_forward(layer_low.astype(jnp.float32), places, weights)
        sent_rows = result.astype(jnp.bfloat16)
        results.append(sent_rows)
        kept_list.append(kept_state)
        inputs_list.append(layer_low)
        if moment < micro_count:
            arrived = shifted(sent_rows, "section", 1)
    forward_stack = jnp.stack(results)
    layer_out = lax.dynamic_slice_in_dim(forward_stack, section_index, micro_count, 0)
    gathered = (
        lax.all_gather(first_gain, "fsdp", axis=1, tiled=True),
        lax.all_gather(first_bias, "fsdp", axis=1, tiled=True),
        lax.all_gather(second_gain, "fsdp", axis=1, tiled=True),
        lax.all_gather(second_bias, "fsdp", axis=1, tiled=True),
        lax.all_gather(qkv_weight, "fsdp", axis=1, tiled=True),
        lax.all_gather(qkv_bias, "fsdp", axis=1, tiled=True),
        lax.all_gather(dense_weight, "fsdp", axis=1, tiled=True),
        lax.all_gather(dense_bias, "fsdp", axis=1, tiled=True),
        lax.all_gather(expand_weight, "fsdp", axis=1, tiled=True),
        lax.all_gather(expand_bias, "fsdp", axis=1, tiled=True),
        lax.all_gather(shrink_weight, "fsdp", axis=1, tiled=True),
        lax.all_gather(shrink_bias, "fsdp", axis=1, tiled=True),
    )
    weights = tuple((member[0] for member in gathered))
    kept_stack = jax.tree.map(stack_all, *kept_list)
    inputs_stack = jnp.stack(inputs_list)
    returned = jnp.zeros((tok_count, width), jnp.bfloat16)
    summed = None
    back_results = []
    for moment in range(micro_count + 1):
        number = moment - 1 + section_index
        valid_flag = ((number >= 0) & (number < micro_count)).astype(jnp.float32)
        index_here = jnp.clip(number, 0, micro_count - 1)
        tick_slot = jnp.clip(number + section_index, 0, micro_count)
        places = lax.dynamic_index_in_dim(own_places, index_here, 0, keepdims=False)
        layer_in = pick_slot(tick_slot, inputs_stack).astype(jnp.float32)
        kept_state = jax.tree.map(partial(pick_slot, tick_slot), kept_stack)
        out_grad = jnp.where(is_first, returned, own_seeds[min(moment, micro_count - 1)])
        input_grad, layer_grads = layer_backward(layer_in, places, weights, kept_state, out_grad)
        layer_grads = tuple((member * valid_flag for member in layer_grads))
        summed = layer_grads if summed is None else jax.tree.map(jnp.add, summed, layer_grads)
        sent_rows = input_grad.astype(jnp.bfloat16)
        back_results.append(sent_rows)
        if moment < micro_count:
            returned = shifted(sent_rows, "section", -1)
    backward_stack = jnp.stack(back_results)
    grad_rows = lax.dynamic_slice_in_dim(backward_stack, 1 - section_index, micro_count, 0)
    lifted = tuple((member[None] for member in summed))
    spread = (
        lax.psum_scatter(
            lifted[0].astype(jnp.bfloat16), "fsdp", scatter_dimension=1, tiled=True
        ).astype(jnp.float32),
        lax.psum_scatter(
            lifted[1].astype(jnp.bfloat16), "fsdp", scatter_dimension=1, tiled=True
        ).astype(jnp.float32),
        lax.psum_scatter(
            lifted[2].astype(jnp.bfloat16), "fsdp", scatter_dimension=1, tiled=True
        ).astype(jnp.float32),
        lax.psum_scatter(
            lifted[3].astype(jnp.bfloat16), "fsdp", scatter_dimension=1, tiled=True
        ).astype(jnp.float32),
        lax.psum_scatter(
            lifted[4].astype(jnp.bfloat16), "fsdp", scatter_dimension=1, tiled=True
        ).astype(jnp.float32),
        lax.psum_scatter(
            lifted[5].astype(jnp.bfloat16), "fsdp", scatter_dimension=1, tiled=True
        ).astype(jnp.float32),
        lax.psum_scatter(
            lifted[6].astype(jnp.bfloat16), "fsdp", scatter_dimension=1, tiled=True
        ).astype(jnp.float32),
        lax.psum_scatter(
            lifted[7].astype(jnp.bfloat16), "fsdp", scatter_dimension=1, tiled=True
        ).astype(jnp.float32),
        lax.psum_scatter(
            lifted[8].astype(jnp.bfloat16), "fsdp", scatter_dimension=1, tiled=True
        ).astype(jnp.float32),
        lax.psum_scatter(
            lifted[9].astype(jnp.bfloat16), "fsdp", scatter_dimension=1, tiled=True
        ).astype(jnp.float32),
        lax.psum_scatter(
            lifted[10].astype(jnp.bfloat16), "fsdp", scatter_dimension=1, tiled=True
        ).astype(jnp.float32),
        lax.psum_scatter(
            lifted[11].astype(jnp.bfloat16), "fsdp", scatter_dimension=1, tiled=True
        ).astype(jnp.float32),
    )
    shards = (
        lax.psum(spread[0].astype(jnp.bfloat16), "seq").astype(jnp.float32),
        lax.psum(spread[1].astype(jnp.bfloat16), "seq").astype(jnp.float32),
        lax.psum(spread[2].astype(jnp.bfloat16), "seq").astype(jnp.float32),
        lax.psum(spread[3].astype(jnp.bfloat16), "seq").astype(jnp.float32),
        lax.psum(spread[4].astype(jnp.bfloat16), "seq").astype(jnp.float32),
        lax.psum(spread[5].astype(jnp.bfloat16), "seq").astype(jnp.float32),
        lax.psum(spread[6].astype(jnp.bfloat16), "seq").astype(jnp.float32),
        lax.psum(spread[7].astype(jnp.bfloat16), "seq").astype(jnp.float32),
        lax.psum(spread[8].astype(jnp.bfloat16), "seq").astype(jnp.float32),
        lax.psum(spread[9].astype(jnp.bfloat16), "seq").astype(jnp.float32),
        lax.psum(spread[10].astype(jnp.bfloat16), "seq").astype(jnp.float32),
        lax.psum(spread[11].astype(jnp.bfloat16), "seq").astype(jnp.float32),
    )
    out_shape = (1, micro_count, 1, tok_count, width)
    return (
        layer_out.reshape(out_shape),
        grad_rows.reshape(out_shape),
        shards[0],
        shards[1],
        shards[2],
        shards[3],
        shards[4],
        shards[5],
        shards[6],
        shards[7],
        shards[8],
        shards[9],
        shards[10],
        shards[11],
    )


def solution(mesh):
    placed = (
        P(None, "fsdp", "seq", None),
        P(None, "fsdp", "seq", None),
        P(None, "fsdp", "seq"),
        P("section", "fsdp"),
        P("section", "fsdp"),
        P("section", "fsdp"),
        P("section", "fsdp"),
        P("section", "fsdp", None),
        P("section", "fsdp"),
        P("section", "fsdp", None),
        P("section", "fsdp"),
        P("section", "fsdp", None),
        P("section", "fsdp"),
        P("section", "fsdp", None),
        P("section", "fsdp"),
    )
    return jax.shard_map(
        on_device,
        mesh=mesh,
        in_specs=placed,
        out_specs=(
            P("section", None, "fsdp", "seq", None),
            P("section", None, "fsdp", "seq", None),
            P("section", "fsdp"),
            P("section", "fsdp"),
            P("section", "fsdp"),
            P("section", "fsdp"),
            P("section", "fsdp", None),
            P("section", "fsdp"),
            P("section", "fsdp", None),
            P("section", "fsdp"),
            P("section", "fsdp", None),
            P("section", "fsdp"),
            P("section", "fsdp", None),
            P("section", "fsdp"),
        ),
        check_vma=False,
    )
```

profile of v0, /device:TPU:0, one launch (start us, length us, event | category | flops | bytes accessed | tf_op | source)
XLA Modules:
  0.0 989.9 jit_solution(8277520707081912004)
XLA Ops:
  20.2 76.0 %all-reduce.15 = (bf16[3072]{0:T(1024)(128)(2,1)S(1)}, bf16[768]{0:T(1024)(128)(2,1)S(1)}, bf16[768]{0:T(1024)(128)(2,1)S(1)}, bf16[2304]{0:T(1024)(128)(2,1)S(1...) all-reduce(bf16[3072]{0:T(1024)(128)(2,1)S(1)} %dynamic-update-slic, ...), channel_id=1, replica_groups=mesh['section'=2,'seq'=4,'fsdp'=16] {'fsdp'}, use_global_device_ids=true, to_apply=%add.6 | all-reduce | flops 9984 | bytes 39936
  122.0 4.8 all-to-all-start
  128.4 5.2 all-to-all-done
  141.2 5.3 all-to-all-done.1
  148.1 13.9 %all-gather.9.cloned.1.call-done = bf16[1,768,3072]{2,1,0:T(8,128)(2,1)} async-done(((bf16[1,48,3072]{2,1,0:T(8,128)(2,1)}), bf16[1,768,3072]{2,1,0:T(8,128)(2,1)}) %all-gather.9.cloned.1.call-update) | async-done | bytes 4718608 | tf_op jit(solution)/shard_map/all_gather | solution.py:304
  166.3 51.5 %all-gather.11.cloned.1.call-done = bf16[1,3072,768]{2,1,0:T(8,128)(2,1)} async-done(((bf16[1,192,768]{2,1,0:T(8,128)(2,1)}), bf16[1,3072,768]{2,1,0:T(8,128)(2,1)}) %all-gather.11.cloned.1.call-update) | async-done | bytes 4718608 | tf_op jit(solution)/shard_map/all_gather | solution.py:306
  217.9 4.9 fusion.10
  265.2 5.3 fusion.8
  288.7 5.0 all-to-all-start.3
  410.8 5.0 all-to-all-start.7
  468.2 5.9 convert_reduce_fusion.1
  480.8 4.8 all-to-all-start.9
  488.4 7.4 all-to-all-done.9
  530.7 6.0 convert_reduce_fusion
  569.8 5.9 all-to-all-done.11
  607.8 8.7 fusion.24
  622.7 5.5 fusion.26
  638.4 5.4 fusion.6
  652.1 72.8 %all-reduce.14 = (bf16[1,768]{1,0:T(2,128)(2,1)S(1)}, bf16[1,768]{1,0:T(2,128)(2,1)S(1)}, bf16[1,768]{1,0:T(2,128)(2,1)S(1)}, bf16[1,768]{1,0:T(2,128)(2,1)S(1)}...) all-reduce(bf16[1,768]{1,0:T(2,128)(2,1)S(1)} %convert_element_type, ...), channel_id=2, replica_groups=mesh['section'=2,'seq'=4,'fsdp'=16] {'fsdp'}, use_global_device_ids=true, to_apply=%region_36.37.clone | all-reduce | flops 6144 | bytes 24576
  725.2 41.1 %reduce-scatter.14.cloned.1.call-done = bf16[1,48,2304]{2,1,0:T(8,128)(2,1)} async-done(((bf16[1,768,2304]{2,1,0:T(8,128)(2,1)}), bf16[1,48,2304]{2,1,0:T(8,128)(2,1)}) %reduce-scatter.14.cloned.1.call-update) | async-done | bytes 221200 | tf_op jit(solution)/shard_map/reduce_scatter | solution.py:383
  766.4 80.9 %reduce-scatter.20.cloned.1.call-done = bf16[1,192,768]{2,1,0:T(8,128)(2,1)} async-done(((bf16[1,3072,768]{2,1,0:T(8,128)(2,1)}), bf16[1,192,768]{2,1,0:T(8,128)(2,1)}) %reduce-scatter.20.cloned.1.call-update) | async-done | bytes 294928 | tf_op jit(solution)/shard_map/reduce_scatter | solution.py:401
  847.2 81.1 %reduce-scatter.18.cloned.1.call-done = bf16[1,48,3072]{2,1,0:T(8,128)(2,1)} async-done(((bf16[1,768,3072]{2,1,0:T(8,128)(2,1)}), bf16[1,48,3072]{2,1,0:T(8,128)(2,1)}) %reduce-scatter.18.cloned.1.call-update) | async-done | bytes 294928 | tf_op jit(solution)/shard_map/reduce_scatter | solution.py:395
  928.4 10.5 %all-reduce.16 = (bf16[1,48]{1,0:T(2,128)(2,1)S(1)}, bf16[1,48]{1,0:T(2,128)(2,1)S(1)}, bf16[1,48]{1,0:T(2,128)(2,1)S(1)}, bf16[1,48]{1,0:T(2,128)(2,1)S(1)}, bf...) all-reduce(bf16[1,48]{1,0:T(2,128)(2,1)S(1)} %constant_dynamic-slic, ...), channel_id=1, replica_groups=mesh['section'=2,'seq'=4,'fsdp'=16] {'seq'}, use_global_device_ids=true, to_apply=%region_37.38 | all-reduce | flops 576 | bytes 2304 | tf_op jit(solution)/shard_map/psum | solution.py:409
  943.2 32.0 %all-reduce.20.cloned.1.call-done = (bf16[1,48,2304]{2,1,0:T(8,128)(2,1)}, bf16[1,48,768]{2,1,0:T(8,128)(2,1)}, bf16[1,48,3072]{2,1,0:T(8,128)(2,1)}, bf16[1,192,768]{2,1,0:T(8,128)(2,1)}) async-done(((bf16[1,48,2304]{2,1,0:T(8,128)(2,1)}, bf16[1,48,768]{2,1,0:T(8,128)(2,1)}, bf16[1,48,3072]{2,1,0:T(8,128)(2,1)}, bf16[1,192,768]{2,1,0:T(8,128)(2,1)}), (bf16[1,48,2304]{2,1,0:T(8,128)(2,1)}, ...) | async-done | bytes 884752 | tf_op jit(solution)/shard_map/psum | solution.py:413
  (676 shorter events, 424.8 us)
Async XLA Ops:
  7.2 100.6 %all-gather.7.cloned.1.call-start = ((), (), s32[]{:S(2)}) async-start(), calls=%async_computation.18 | async-start | bytes 1253376 | tf_op jit(solution)/shard_map/all_gather | solution.py:302
  7.9 106.9 %all-gather.5.cloned.1.call-start = ((), (), s32[]{:S(2)}) async-start(), calls=%async_computation.17 | async-start | bytes 3760128 | tf_op jit(solution)/shard_map/all_gather | solution.py:300
  8.7 153.4 %all-gather.9.cloned.1.call-start = ((), (), s32[]{:S(2)}) async-start(), calls=%async_computation.19 | async-start | bytes 5013504 | tf_op jit(solution)/shard_map/all_gather | solution.py:304
  9.4 208.5 %all-gather.11.cloned.1.call-start = ((), (), s32[]{:S(2)}) async-start(), calls=%async_computation.20 | async-start | bytes 5013504 | tf_op jit(solution)/shard_map/all_gather | solution.py:306
  110.4 11.6 %all-to-all-start.6 = ((bf16[64,4,192]{2,0,1:T(8,128)(2,1)}), bf16[64,4,192]{2,0,1:T(8,128)(2,1)S(1)}, u32[]{:S(2)}, u32[]{:S(2)}) async-start(bf16[64,4,192]{2,0,1:T(8,128)(2,1)} %copy.303), calls=%async_computation.6 | async-start | bytes 262144 | tf_op jit(solution)/shard_map/all_to_all | solution.py:221
  122.0 11.7 %all-to-all-start = ((bf16[4,2,18432]{2,1,0:T(2,128)(2,1)}), bf16[4,2,18432]{2,1,0:T(2,128)(2,1)S(1)}, u32[]{:S(2)}, u32[]{:S(2)}) async-start(bf16[4,2,18432]{2,1,0:T(2,128)(2,1)} %reshape.1466), calls=%async_computation | async-start | bytes 589824 | tf_op jit(solution)/shard_map/all_to_all | solution.py:168
  136.8 9.7 all-to-all-start.1
  256.6 13.8 %all-to-all-start.2 = ((bf16[4,2,18432]{2,1,0:T(2,128)(2,1)}), bf16[4,2,18432]{2,1,0:T(2,128)(2,1)}, u32[]{:S(2)}, u32[]{:S(2)}) async-start(bf16[4,2,18432]{2,1,0:T(2,128)(2,1)} %reshape.1468), calls=%async_computation.2 | async-start | bytes 589824 | tf_op jit(solution)/shard_map/all_to_all | solution.py:168
  288.7 11.0 %all-to-all-start.3 = ((bf16[4,64,192]{2,1,0:T(8,128)(2,1)}), bf16[4,64,192]{2,1,0:T(8,128)(2,1)}, u32[]{:S(2)}, u32[]{:S(2)}) async-start(bf16[4,64,192]{2,1,0:T(8,128)(2,1)} %copy.289), calls=%async_computation.3 | async-start | bytes 262144 | tf_op jit(solution)/shard_map/all_to_all | solution.py:170
  341.6 18.1 %all-to-all-start.4 = ((bf16[4,2,18432]{2,1,0:T(2,128)(2,1)}), bf16[4,2,18432]{2,1,0:T(2,128)(2,1)}, u32[]{:S(2)}, u32[]{:S(2)}) async-start(bf16[4,2,18432]{2,1,0:T(2,128)(2,1)} %reshape.1470), calls=%async_computation.4 | async-start | bytes 589824 | tf_op jit(solution)/shard_map/all_to_all | solution.py:168
  390.7 20.1 %all-to-all-start.5 = ((bf16[4,64,192]{2,1,0:T(8,128)(2,1)}), bf16[4,64,192]{2,1,0:T(8,128)(2,1)}, u32[]{:S(2)}, u32[]{:S(2)}) async-start(bf16[4,64,192]{2,1,0:T(8,128)(2,1)} %copy.300), calls=%async_computation.5 | async-start | bytes 262144 | tf_op jit(solution)/shard_map/all_to_all | solution.py:170
  410.8 13.6 %all-to-all-start.7 = ((bf16[256,3,192]{2,1,0:T(4,128)(2,1)}), bf16[256,3,192]{2,1,0:T(4,128)(2,1)}, u32[]{:S(2)}, u32[]{:S(2)}) async-start(bf16[256,3,192]{2,1,0:T(4,128)(2,1)} %pad_maximum_fusion.2), calls=%async_computation.7 | async-start | bytes 1048576 | tf_op jit(solution)/shard_map/all_to_all | solution.py:225
  456.4 5.5 collective-permute-start.2
  463.9 12.5 %all-to-all-start.8 = ((bf16[64,4,192]{2,0,1:T(8,128)(2,1)}), bf16[64,4,192]{2,0,1:T(8,128)(2,1)S(1)}, u32[]{:S(2)}, u32[]{:S(2)}) async-start(bf16[64,4,192]{2,0,1:T(8,128)(2,1)} %copy.317), calls=%async_computation.8 | async-start | bytes 262144 | tf_op jit(solution)/shard_map/all_to_all | solution.py:221
  480.8 15.0 %all-to-all-start.9 = ((bf16[256,3,192]{2,1,0:T(4,128)(2,1)}), bf16[256,3,192]{2,1,0:T(4,128)(2,1)S(1)}, u32[]{:S(2)}, u32[]{:S(2)}) async-start(bf16[256,3,192]{2,1,0:T(4,128)(2,1)} %pad_maximum_fusion.3), calls=%async_computation.9 | async-start | bytes 1048576 | tf_op jit(solution)/shard_map/all_to_all | solution.py:225
  515.2 5.7 collective-permute-start.3
  526.6 15.6 %all-to-all-start.10 = ((bf16[64,4,192]{2,0,1:T(8,128)(2,1)}), bf16[64,4,192]{2,0,1:T(8,128)(2,1)}, u32[]{:S(2)}, u32[]{:S(2)}) async-start(bf16[64,4,192]{2,0,1:T(8,128)(2,1)} %copy.331), calls=%async_computation.10 | async-start | bytes 262144 | tf_op jit(solution)/shard_map/all_to_all | solution.py:221
  530.6 117.6 %reduce-scatter.22.cloned.1.call-start = ((), (), s32[]{:S(2)}) async-start(), calls=%async_computation.25 | async-start | bytes 835584
  538.1 187.2 %reduce-scatter.16.cloned.1.call-start = ((), (), s32[]{:S(2)}) async-start(), calls=%async_computation.22 | async-start | bytes 1253376 | tf_op jit(solution)/shard_map/reduce_scatter | solution.py:389
  560.4 15.3 %all-to-all-start.11 = ((bf16[256,3,192]{2,1,0:T(4,128)(2,1)}), bf16[256,3,192]{2,1,0:T(4,128)(2,1)}, u32[]{:S(2)}, u32[]{:S(2)}) async-start(bf16[256,3,192]{2,1,0:T(4,128)(2,1)} %pad_maximum_fusion.4), calls=%async_computation.11 | async-start | bytes 1048576 | tf_op jit(solution)/shard_map/all_to_all | solution.py:225
  565.0 201.3 %reduce-scatter.14.cloned.1.call-start = ((), (), s32[]{:S(2)}) async-start(), calls=%async_computation.21 | async-start | bytes 3760128 | tf_op jit(solution)/shard_map/reduce_scatter | solution.py:383
  616.5 230.8 %reduce-scatter.20.cloned.1.call-start = ((), (), s32[]{:S(2)}) async-start(), calls=%async_computation.24 | async-start | bytes 5013504 | tf_op jit(solution)/shard_map/reduce_scatter | solution.py:401
  628.3 300.0 %reduce-scatter.18.cloned.1.call-start = ((), (), s32[]{:S(2)}) async-start(), calls=%async_computation.23 | async-start | bytes 5013504 | tf_op jit(solution)/shard_map/reduce_scatter | solution.py:395
  636.5 338.7 %all-reduce.20.cloned.1.call-start = ((), (), s32[]{:S(2)}) async-start(), calls=%async_computation.26 | async-start | bytes 1769472 | tf_op jit(solution)/shard_map/psum | solution.py:413
  (133 other events, 2698.9 us)
Sparse Core Ops, SparseCore 0:
  10.2 45.6 all-gather.6
  58.1 48.6 all-gather.4
  109.0 53.0 all-gather.8
  164.1 53.6 all-gather.10
  538.2 73.2 reduce-scatter.21
  614.5 72.5 reduce-scatter.15
  690.6 75.7 reduce-scatter.13
  769.7 77.4 reduce-scatter.19
  850.6 77.6 reduce-scatter.17
  930.8 44.3 all-reduce.19
where the time goes:
time: 1000 us; the launch traced here: 990 us
  waiting for transfers between devices  333 us (33%)
  local copies, waits for them, and re-layouts  185 us (18%)
  blocking collectives  159 us (16%)
  matrix products  139 us (14%)
  other arithmetic  93.2 us (9%)
  starting transfers between devices  60.7 us (6%)
  between operations  20.1 us (2%)
    unnamed x2, blocking collectives  149 us
    reduce_scatter x1, waiting for transfers between devices, on_device(): lax.psum_scatter(lifted[8].astype(jnp.bfloat16), 'fsdp', scatter_dimensio...  81.1 us
    reduce_scatter x1, waiting for transfers between devices, on_device(): lax.psum_scatter(lifted[10].astype(jnp.bfloat16), 'fsdp', scatter_dimensi...  80.9 us
    all_gather x1, waiting for transfers between devices, on_device(): lax.all_gather(shrink_weight, 'fsdp', axis=1, tiled=True)  51.5 us
    dot_general x12, matrix products, contract_rows(): lax.dot_general(left_side, right_side, (((0,), (0,)), ((), ())), preferre...  45.1 us
    reduce_scatter x1, waiting for transfers between devices, on_device(): lax.psum_scatter(lifted[4].astype(jnp.bfloat16), 'fsdp', scatter_dimensio...  41.1 us
    dot_general x12, matrix products, contract_cols(): lax.dot_general(left_side, right_side, (((1,), (1,)), ((), ())), preferre...  37 us
    dot_general x12, matrix products, matmul_f32(): return jnp.dot(left_side, right_side, preferred_element_type=jnp.float32)  36.9 us
  transfers between devices with their start and end apart: 26, of which 13 were waited for; matrix products, arithmetic and copies ran while one was open for 22% of the time, Pallas kernels for 0%

commit v1 on v0

v1 whole, which is shorter than its diff:
```python
import math

import jax
import jax.numpy as jnp
import numpy as np
from jax import lax
from jax.experimental import pallas as pl
from jax.experimental.pallas import tpu as pltpu
from jax.sharding import PartitionSpec as P

MESH = pl.DeviceIdType.MESH
F32 = jnp.float32
BF16 = jnp.bfloat16
HD = 64
ROT = 16
WIDTH = 768
TOK = 64
LEN = 256
GROUP = 192
NEAR = (1, 3, 2)
MIB = 1024 * 1024

KINDS = ((48, 576, False), (48, 768, True), (48, 768, False), (16, 128, True))


def ring(value, by):
    return lax.rem(value + by, 4)


def places():
    owner = lax.axis_index("fsdp")
    return owner, lax.div(owner, 4), lax.rem(owner, 4)


def joined(u, v, x_first):
    return u * 4 + v if x_first else v * 4 + u


def remote(src, dst, send, recv, target):
    return pltpu.make_async_remote_copy(
        src_ref=src, dst_ref=dst, send_sem=send, recv_sem=recv, device_id=target, device_id_type=MESH
    )


def greet(targets):
    barrier = pltpu.get_barrier_semaphore()
    for target in targets:
        pl.semaphore_signal(barrier, inc=1, device_id=target, device_id_type=MESH)
    pl.semaphore_wait(barrier, len(targets))


def sheet_peers(x, z):
    return [{"fsdp": ring(x, d) * 4 + z} for d in (1, 2, 3)] + [
        {"fsdp": x * 4 + ring(z, d)} for d in (1, 2, 3)
    ]


def seq_peers(y):
    return [{"seq": ring(y, d)} for d in (1, 2, 3)]


def dot(a, b):
    return jnp.dot(a, b, preferred_element_type=F32)


def dot_nt(a, b):
    return lax.dot_general(a, b, (((1,), (1,)), ((), ())), preferred_element_type=F32)


def dot_tn(a, b):
    return lax.dot_general(a, b, (((0,), (0,)), ((), ())), preferred_element_type=F32)


def gather_kernel(*refs):
    shards, dense = refs[0:4], refs[4]
    wholes, dense_whole = refs[5:9], refs[9]
    send, recv, own_sem, dsend, drecv, csend, crecv = refs[10:]
    layer = lax.axis_index("section")
    y = lax.axis_index("seq")
    owner, x, z = places()
    sibling = {"section": 1 - layer}
    greet(sheet_peers(x, z) + [sibling])

    def slot(t, s):
        rows = KINDS[t][0]
        return wholes[t].at[layer, pl.ds(pl.multiple_of(s * rows, 16), rows), :]

    def band(i):
        return dense_whole.at[layer, pl.ds(pl.multiple_of(i * 48, 16), 48), :]

    order = (0, 3, 1, 2)
    sent = []
    for t in order:
        x_first = KINDS[t][2]
        u, v = (x, z) if x_first else (z, x)
        pltpu.make_async_copy(shards[t], slot(t, owner), own_sem.at[t]).start()
        for k, d in enumerate(NEAR):
            copy = remote(
                shards[t],
                slot(t, owner),
                send.at[t, k],
                recv.at[t, owner],
                {"fsdp": joined(ring(u, d), v, x_first)},
            )
            copy.start()
            sent.append(copy)

    holds = x == y

    @pl.when(holds)
    def _():
        pltpu.make_async_copy(dense, band(z), own_sem.at[4]).start()
        for k, d in enumerate(NEAR):
            remote(
                dense, band(z), dsend.at[k], drecv.at[z], {"fsdp": ring(x, d) * 4 + z}
            ).start()

    for t in order:
        x_first = KINDS[t][2]
        u, v = (x, z) if x_first else (z, x)
        for d in (0, 1, 3, 2):
            s = joined(ring(u, 4 - d), v, x_first)
            if d:
                remote(shards[t], slot(t, s), send.at[t, 0], recv.at[t, s], sibling).wait_recv()
            for k, e in enumerate(NEAR):
                copy = remote(
                    slot(t, s) if d else shards[t],
                    slot(t, s),
                    send.at[t, 3 + 3 * d + k],
                    recv.at[t, s],
                    {"fsdp": joined(u, ring(v, e), x_first)},
                )
                copy.start()
                sent.append(copy)

    @pl.when(holds)
    def _():
        pltpu.make_async_copy(dense, band(z), own_sem.at[4]).wait()

    @pl.when(jnp.logical_not(holds))
    def _():
        remote(dense, band(z), dsend.at[0], drecv.at[z], sibling).wait_recv()

    dense_sent = []
    for k, e in enumerate(NEAR):
        copy = remote(
            band(z), band(z), dsend.at[3 + k], drecv.at[z], {"fsdp": x * 4 + ring(z, e)}
        )
        copy.start()
        dense_sent.append(copy)

    across = []
    for t in order:
        x_first = KINDS[t][2]
        u, v = (x, z) if x_first else (z, x)
        pltpu.make_async_copy(shards[t], slot(t, owner), own_sem.at[t]).wait()
        for e in NEAR:
            for d in (0, 1, 3, 2):
                s = joined(ring(u, 4 - d), ring(v, 4 - e), x_first)
                remote(shards[t], slot(t, s), send.at[t, 0], recv.at[t, s], sibling).wait_recv()
        copy = remote(wholes[t].at[layer], wholes[t].at[layer], csend.at[t], crecv.at[t], sibling)
        copy.start()
        across.append(copy)
    for e in NEAR:
        i = ring(z, 4 - e)
        remote(dense, band(i), dsend.at[0], drecv.at[i], sibling).wait_recv()
    copy = remote(dense_whole.at[layer], dense_whole.at[layer], csend.at[4], crecv.at[4], sibling)
    copy.start()
    across.append(copy)

    for copy in sent + dense_sent:
        copy.wait_send()

    @pl.when(holds)
    def _():
        for k in range(3):
            remote(dense, band(z), dsend.at[k], drecv.at[z], sibling).wait_send()

    for t, copy in enumerate(across):
        copy.wait_send()
    for t in range(5):
        whole = wholes[t] if t < 4 else dense_whole
        remote(whole.at[layer], whole.at[1 - layer], csend.at[t], crecv.at[t], sibling).wait_recv()


def gather_weights(shards, dense):
    hbm = pl.BlockSpec(memory_space=pl.ANY)
    dma = pltpu.SemaphoreType.DMA
    return pl.pallas_call(
        gather_kernel,
        out_shape=[jax.ShapeDtypeStruct((2, 16 * rows, cols), BF16) for rows, cols, _ in KINDS]
        + [jax.ShapeDtypeStruct((2, GROUP, WIDTH), BF16)],
        in_specs=[hbm] * 5,
        out_specs=[hbm] * 5,
        scratch_shapes=[dma((4, 15)), dma((4, 16)), dma((5,)), dma((6,)), dma((4,)), dma((5,)), dma((5,))],
        compiler_params=pltpu.CompilerParams(collective_id=1, has_side_effects=True),
        name="gather_weights",
    )(*shards, dense)


def turn_tables(tab_ref, odd, sign):
    tables = []
    for i in range(3):
        table = jnp.where(odd, tab_ref[3 + i], tab_ref[i])
        if i and sign < 0:
            table = -table
        tables.append(jnp.concatenate([table] * 3, axis=1))
    return tables


def turn(values, tables):
    cosine, low_sine, high_sine = tables
    span = values.shape[1]
    return (
        values * cosine
        + pltpu.roll(values, span - 8, 1) * low_sine
        + pltpu.roll(values, 8, 1) * high_sine
    )


def column_block(shape):
    col = lax.broadcasted_iota(jnp.int32, shape, 1)
    return lax.shift_right_logical(col * 43691, 21)


def piece_mask(shape):
    row = lax.broadcasted_iota(jnp.int32, shape, 0)
    return lax.shift_right_logical(row, 4) == column_block(shape)


def joint_mask(shape, y):
    row = lax.broadcasted_iota(jnp.int32, shape, 0)
    k = (row & 15) - 7
    chunk = 3 * lax.shift_right_logical(row, 4) + k
    block = column_block(shape)
    wanted = 16 * lax.shift_right_logical(block, 2) + (block & 3) + 4 * y
    return (k >= 0) & (k < 3) & (chunk == wanted)


def spread_matrix():
    shape = (128, WIDTH)
    col = lax.broadcasted_iota(jnp.int32, shape, 1)
    row = lax.broadcasted_iota(jnp.int32, shape, 0)
    return jnp.where(col - 48 * column_block(shape) == row, 1.0, 0.0).astype(BF16)


def layers_kernel(
    x_ref, cot_ref, pos_ref, tab_ref, wq, we, ws, vec, wd,
    lo_out, ig_out, dq_out, de_out, ds_out, dv_out, dd_out,
    xall, dyall, posall, part, psend, prec, qkvs, probs, ctx, acts, slopes,
    n1s, n2s, xhs, vrows, bqs, grows, cur, staged, arrived,
    asend, arecv, rsend, rrecv, posend, porecv, csend, crecv,
):
    micro = lax.axis_index("section")
    y = lax.axis_index("seq")
    sibling = {"section": 1 - micro}
    greet(seq_peers(y) + [sibling])
    own = pl.ds(pl.multiple_of(y * TOK, TOK), TOK)

    def rows_of(i):
        return pl.ds(pl.multiple_of(i * TOK, TOK), TOK)

    def share(ref, sends, recvs):
        copies = []
        for k, d in enumerate(NEAR):
            copy = remote(ref.at[own, :], ref.at[own, :], sends.at[k], recvs.at[k], {"seq": ring(y, d)})
            copy.start()
            copies.append(copy)
        return copies

    def collect(ref, copies, sends, recvs):
        for k, d in enumerate(NEAR):
            src = ref.at[rows_of(ring(y, 4 - d)), :]
            remote(src, src, sends.at[k], recvs.at[k], sibling).wait_recv()
        for copy in copies:
            copy.wait_send()

    def reduce_rows(value, back, l):
        part[...] = value
        psend[back, l] = value.astype(BF16)
        copies = []
        for k, d in enumerate(NEAR):
            to = ring(y, d)
            copy = remote(
                psend.at[back, l, rows_of(to), :],
                prec.at[back, l, k],
                rsend.at[back, l, k],
                rrecv.at[back, l, k],
                {"seq": to},
            )
            copy.start()
            copies.append(copy)
        for copy in copies:
            copy.wait()
        total = part[own, :]
        for k in range(3):
            total = total + prec[back, l, k].astype(F32)
        return total

    posall[own, :] = pos_ref[...]
    pos_copies = share(posall, posend, porecv)

    spread = spread_matrix()
    pieces = piece_mask((LEN, WIDTH))
    joints = joint_mask((LEN, 3 * GROUP), y)
    for l in range(2):
        columns = dot(vec[l], spread)
        vrows[l] = jnp.sum(
            jnp.where(pieces, columns, 0.0).reshape(16, 16, WIDTH), axis=0
        )
        bqs[l] = jnp.broadcast_to(
            jnp.sum(jnp.where(joints, columns[:, : 3 * GROUP], 0.0), axis=0, keepdims=True),
            (8, 3 * GROUP),
        )
    cur[...] = x_ref[...]
    collect(posall, pos_copies, posend, porecv)
    token = lax.broadcasted_iota(jnp.int32, (LEN, 128), 0)
    odd = posall[...] > 2 * token

    def forward(l, carry):
        xall[l, own, :] = cur[...]
        here = xall.at[l]
        collect(here, share(here, asend.at[0, l], arecv.at[0, l]), asend.at[0, l], arecv.at[0, l])
        values = xall[l].astype(F32)
        center = values - jnp.mean(values, axis=-1, keepdims=True)
        scale = lax.rsqrt(jnp.mean(center * center, axis=-1, keepdims=True) + 1e-5)
        normed = center * scale
        xhs[l] = normed
        n1 = (normed * vrows[l, 0:1, :] + vrows[l, 1:2, :]).astype(BF16)
        n2 = (normed * vrows[l, 2:3, :] + vrows[l, 3:4, :]).astype(BF16)
        n1s[l] = n1
        n2s[l] = n2
        joint = dot(n1, wq[l]) + bqs[l, 0:1, :]
        turned = turn(joint[:, : 2 * GROUP], turn_tables(tab_ref, odd, 1))
        qkvs[l, :, : 2 * GROUP] = turned.astype(BF16)
        qkvs[l, :, 2 * GROUP :] = joint[:, 2 * GROUP :].astype(BF16)
        row = lax.broadcasted_iota(jnp.int32, (LEN, LEN), 0)
        allowed = row >= lax.broadcasted_iota(jnp.int32, (LEN, LEN), 1)
        for n in range(3):
            q = qkvs[l, :, n * HD : (n + 1) * HD]
            k = qkvs[l, :, GROUP + n * HD : GROUP + (n + 1) * HD]
            v = qkvs[l, :, 2 * GROUP + n * HD : 2 * GROUP + (n + 1) * HD]
            scores = jnp.where(allowed, dot_nt(q, k) * HD**-0.5, -1e30)
            powers = jnp.exp(scores - jnp.max(scores, axis=-1, keepdims=True))
            prob = powers / jnp.sum(powers, axis=-1, keepdims=True)
            probs[l, n] = prob
            ctx[l, :, n * HD : (n + 1) * HD] = dot(prob.astype(BF16), v).astype(BF16)
        hidden = dot(n2, we[l]) + vrows[l, 6:7, :]
        phi = 0.5 + 0.5 * lax.erf(hidden * math.sqrt(0.5))
        acts[l] = (hidden * phi).astype(BF16)
        density = jnp.exp(-0.5 * hidden * hidden) * (1.0 / math.sqrt(2.0 * math.pi))
        slopes[l] = phi + hidden * density
        total = reduce_rows(dot(ctx[l], wd[l]) + dot(acts[l], ws[l]), 0, l)
        result = cur[...].astype(F32) + total + vrows[l, 4:5, :] + vrows[l, 5:6, :]
        cur[...] = result.astype(BF16)
        staged[0, l] = cur[...]
        return carry

    lax.fori_loop(0, 2, forward, 0)
    lo_copy = remote(staged.at[0, 1 - micro], arrived.at[0], csend.at[0], crecv.at[0], sibling)
    lo_copy.start()
    cur[...] = cot_ref[...]

    def backward(i, carry):
        l = 1 - i
        dyall[l, own, :] = cur[...]
        here = dyall.at[l]
        collect(here, share(here, asend.at[1, l], arecv.at[1, l]), asend.at[1, l], arecv.at[1, l])
        out_grad = dyall[l]
        hidden_grad = (dot_nt(out_grad, ws[l]) * slopes[l]).astype(BF16)
        ds_out[l] = dot_tn(acts[l], out_grad).astype(BF16)
        de_out[l] = dot_tn(n2s[l], hidden_grad).astype(BF16)
        n2_grad = dot_nt(hidden_grad, we[l])
        ctx_grad = dot_nt(out_grad, wd[l]).astype(BF16)
        dd_out[l] = dot_tn(ctx[l], out_grad).astype(BF16)
        parts = ([], [], [])
        for n in range(3):
            q = qkvs[l, :, n * HD : (n + 1) * HD]
            k = qkvs[l, :, GROUP + n * HD : GROUP + (n + 1) * HD]
            v = qkvs[l, :, 2 * GROUP + n * HD : 2 * GROUP + (n + 1) * HD]
            up = ctx_grad[:, n * HD : (n + 1) * HD]
            prob = probs[l, n]
            prob_grad = dot_nt(up, v)
            inner = jnp.sum(prob * prob_grad, axis=-1, keepdims=True)
            score_grad = (prob * (prob_grad - inner)).astype(BF16)
            parts[0].append(dot(score_grad, k) * HD**-0.5)
            parts[1].append(dot_tn(score_grad, q) * HD**-0.5)
            parts[2].append(dot_tn(prob.astype(BF16), up))
        turned_grad = jnp.concatenate(parts[0] + parts[1], axis=1).astype(BF16).astype(F32)
        joint_grad = jnp.concatenate(
            [turn(turned_grad, turn_tables(tab_ref, odd, -1))] + parts[2], axis=1
        ).astype(BF16)
        dq_out[l] = dot_tn(n1s[l], joint_grad).astype(BF16)
        n1_grad = dot_nt(joint_grad, wq[l])
        normed = xhs[l]
        grows[...] = jnp.zeros_like(grows)
        grows[0:1, :] = jnp.sum(n1_grad * normed, axis=0, keepdims=True)
        grows[1:2, :] = jnp.sum(n1_grad, axis=0, keepdims=True)
        grows[2:3, :] = jnp.sum(n2_grad * normed, axis=0, keepdims=True)
        grows[3:4, :] = jnp.sum(n2_grad, axis=0, keepdims=True)
        grows[4:5, :] = jnp.sum(cur[...].astype(F32), axis=0, keepdims=True)
        grows[6:7, :] = jnp.sum(hidden_grad.astype(F32), axis=0, keepdims=True)
        joint_bias = jnp.sum(joint_grad.astype(F32), axis=0, keepdims=True)
        spread_now = spread_matrix()
        first = jnp.where(piece_mask((LEN, WIDTH)), jnp.concatenate([grows[...]] * 16, axis=0), 0.0)
        second = jnp.where(
            joint_mask((LEN, 3 * GROUP), y), jnp.broadcast_to(joint_bias, (LEN, 3 * GROUP)), 0.0
        )
        dv_out[l] = (
            dot_nt(first.astype(BF16), spread_now)
            + dot_nt(second.astype(BF16), spread_now[:, : 3 * GROUP])
        ).astype(BF16)
        total = reduce_rows(n1_grad * vrows[l, 0:1, :] + n2_grad * vrows[l, 2:3, :], 1, l)
        values = xall[l, own, :].astype(F32)
        center = values - jnp.mean(values, axis=-1, keepdims=True)
        scale = lax.rsqrt(jnp.mean(center * center, axis=-1, keepdims=True) + 1e-5)
        near = center * scale
        pulled = scale * (
            total
            - jnp.mean(total, axis=-1, keepdims=True)
            - near * jnp.mean(total * near, axis=-1, keepdims=True)
        )
        cur[...] = (cur[...].astype(F32) + pulled).astype(BF16)
        staged[1, l] = cur[...]
        return carry

    lax.fori_loop(0, 2, backward, 0)
    ig_copy = remote(staged.at[1, 1 - micro], arrived.at[1], csend.at[1], crecv.at[1], sibling)
    ig_copy.start()
    lo_copy.wait()
    ig_copy.wait()
    lo_out[micro] = staged[0, micro]
    lo_out[1 - micro] = arrived[0]
    ig_out[micro] = staged[1, micro]
    ig_out[1 - micro] = arrived[1]


def run_layers(tokens, cot, spots, tables, wholes, dense_whole):
    vmem = pl.BlockSpec(memory_space=pltpu.VMEM)
    dma = pltpu.SemaphoreType.DMA
    shapes = (
        [(2, TOK, WIDTH), (2, TOK, WIDTH)]
        + [(2, 16 * rows, cols) for rows, cols, _ in KINDS]
        + [(2, GROUP, WIDTH)]
    )
    return pl.pallas_call(
        layers_kernel,
        out_shape=[jax.ShapeDtypeStruct(shape, BF16) for shape in shapes],
        in_specs=[vmem] * 9,
        out_specs=[vmem] * 7,
        scratch_shapes=[
            pltpu.VMEM((2, LEN, WIDTH), BF16),
            pltpu.VMEM((2, LEN, WIDTH), BF16),
            pltpu.VMEM((LEN, 128), jnp.int32),
            pltpu.VMEM((LEN, WIDTH), F32),
            pltpu.VMEM((2, 2, LEN, WIDTH), BF16),
            pltpu.VMEM((2, 2, 3, TOK, WIDTH), BF16),
            pltpu.VMEM((2, LEN, 3 * GROUP), BF16),
            pltpu.VMEM((2, 3, LEN, LEN), F32),
            pltpu.VMEM((2, LEN, GROUP), BF16),
            pltpu.VMEM((2, LEN, WIDTH), BF16),
            pltpu.VMEM((2, LEN, WIDTH), F32),
            pltpu.VMEM((2, LEN, WIDTH), BF16),
            pltpu.VMEM((2, LEN, WIDTH), BF16),
            pltpu.VMEM((2, LEN, WIDTH), F32),
            pltpu.VMEM((2, 16, WIDTH), F32),
            pltpu.VMEM((2, 8, 3 * GROUP), F32),
            pltpu.VMEM((16, WIDTH), F32),
            pltpu.VMEM((TOK, WIDTH), BF16),
            pltpu.VMEM((2, 2, TOK, WIDTH), BF16),
            pltpu.VMEM((2, TOK, WIDTH), BF16),
            dma((2, 2, 3)),
            dma((2, 2, 3)),
            dma((2, 2, 3)),
            dma((2, 2, 3)),
            dma((3,)),
            dma((3,)),
            dma((2,)),
            dma((2,)),
        ],
        compiler_params=pltpu.CompilerParams(
            collective_id=2, has_side_effects=True, vmem_limit_bytes=60 * MIB
        ),
        name="layers",
    )(tokens, cot, spots, tables, *wholes, dense_whole)


def reduce_kernel(*refs):
    grads, dense_grad = refs[0:4], refs[4]
    outs, dense_out = refs[5:9], refs[9]
    accs, dense_acc = refs[10:14], refs[14]
    sibs, dense_sib = refs[15:19], refs[19]
    wides, dense_wide = refs[20:24], refs[24]
    mids = refs[25:29]
    narrows, dense_narrow = refs[29:33], refs[33]
    ends, dense_end = refs[34:38], refs[38]
    own_sem, csend, crecv, asend, arecv, bsend, brecv, ysend, yrecv = refs[39:]
    layer = lax.axis_index("section")
    y = lax.axis_index("seq")
    owner, x, z = places()
    sibling = {"section": 1 - layer}
    greet(sheet_peers(x, z) + seq_peers(y) + [sibling])
    holds = x == y

    all_grads = list(grads) + [dense_grad]
    all_accs = list(accs) + [dense_acc]
    all_sibs = list(sibs) + [dense_sib]
    order = (2, 1, 4, 0, 3)
    own_copies, sib_copies = {}, {}
    for t in order:
        own_copies[t] = pltpu.make_async_copy(all_grads[t].at[layer], all_accs[t], own_sem.at[t])
        own_copies[t].start()
        sib_copies[t] = remote(
            all_grads[t].at[1 - layer], all_sibs[t], csend.at[t], crecv.at[t], sibling
        )
        sib_copies[t].start()

    sent = []
    for t in order:
        own_copies[t].wait()
        sib_copies[t].wait_recv()
        if t == 4:
            for i in range(4):
                dense_acc[i] = (dense_acc[i].astype(F32) + dense_sib[i].astype(F32)).astype(BF16)
            for k, e in enumerate(NEAR):
                to = ring(z, e)
                copy = remote(
                    dense_acc.at[to], dense_wide.at[k], asend.at[t, k], arecv.at[t, k], {"fsdp": x * 4 + to}
                )
                copy.start()
                sent.append(copy)
            continue
        acc, sib = accs[t], sibs[t]

        def add(i, carry, acc=acc, sib=sib):
            a, b = lax.div(i, 4), lax.rem(i, 4)
            acc[a, b] = (acc[a, b].astype(F32) + sib[a, b].astype(F32)).astype(BF16)
            return carry

        lax.fori_loop(0, 16, add, 0)
        x_first = KINDS[t][2]
        u, v = (x, z) if x_first else (z, x)
        for k, e in enumerate(NEAR):
            to = ring(v, e)
            copy = remote(
                acc.at[:, to] if x_first else acc.at[to],
                wides[t].at[k],
                asend.at[t, k],
                arecv.at[t, k],
                {"fsdp": joined(u, to, x_first)},
            )
            copy.start()
            sent.append(copy)

    last = {}
    for t in order:
        if t == 4:
            for k in range(3):
                remote(dense_acc.at[0], dense_wide.at[k], asend.at[t, k], arecv.at[t, k], sibling).wait_recv()
            total = dense_acc[z].astype(F32)
            for k in range(3):
                total = total + dense_wide[k].astype(F32)
            dense_end[...] = total.astype(BF16)

            @pl.when(jnp.logical_not(holds))
            def _():
                away = lax.rem(x - y + 4, 4)
                remote(
                    dense_end, dense_narrow.at[away - 1], bsend.at[4, 0], brecv.at[4, away - 1], {"fsdp": y * 4 + z}
                ).start()

            continue
        acc = accs[t]
        x_first = KINDS[t][2]
        u, v = (x, z) if x_first else (z, x)
        for k in range(3):
            remote(wides[t].at[k], wides[t].at[k], asend.at[t, k], arecv.at[t, k], sibling).wait_recv()
        for d in (1, 3, 2, 0):
            to = ring(u, d)
            total = acc[to, v].astype(F32) if x_first else acc[v, to].astype(F32)
            for k in range(3):
                total = total + wides[t][k, to].astype(F32)
            if d == 0:
                last[t] = None
            mids[t][to] = total.astype(BF16)
            if d:
                k = NEAR.index(d)
                copy = remote(
                    mids[t].at[to],
                    narrows[t].at[k],
                    bsend.at[t, k],
                    brecv.at[t, k],
                    {"fsdp": joined(to, v, x_first)},
                )
                copy.start()
                sent.append(copy)

    for t in order:
        if t == 4:

            @pl.when(holds)
            def _():
                for k in range(3):
                    remote(dense_end, dense_narrow.at[k], bsend.at[4, 0], brecv.at[4, k], sibling).wait_recv()
                total = dense_end[...].astype(F32)
                for k in range(3):
                    total = total + dense_narrow[k].astype(F32)
                dense_out[...] = total.astype(BF16)
                for k, d in enumerate(NEAR):
                    remote(dense_out, dense_out, ysend.at[4, k], yrecv.at[4, 0], {"seq": ring(y, d)}).start()

            continue
        x_first = KINDS[t][2]
        u, v = (x, z) if x_first else (z, x)
        for k in range(3):
            remote(narrows[t].at[k], narrows[t].at[k], bsend.at[t, k], brecv.at[t, k], sibling).wait_recv()
        total = mids[t][u].astype(F32)
        for k in range(3):
            total = total + narrows[t][k].astype(F32)
        ends[t][y] = total.astype(BF16)
        for k, d in enumerate(NEAR):
            copy = remote(
                ends[t].at[y], ends[t].at[y], ysend.at[t, k], yrecv.at[t, k], {"seq": ring(y, d)}
            )
            copy.start()
            sent.append(copy)

    for t in range(4):
        for k, d in enumerate(NEAR):
            src = ends[t].at[ring(y, 4 - d)]
            remote(src, src, ysend.at[t, k], yrecv.at[t, k], sibling).wait_recv()
        outs[t][...] = ends[t][...]

    @pl.when(holds)
    def _():
        for k in range(3):
            remote(dense_out, dense_out, ysend.at[4, k], yrecv.at[4, 0], sibling).wait_send()

    @pl.when(jnp.logical_not(holds))
    def _():
        remote(dense_out, dense_out, ysend.at[4, 0], yrecv.at[4, 0], sibling).wait_recv()
        remote(dense_end, dense_narrow.at[0], bsend.at[4, 0], brecv.at[4, 0], sibling).wait_send()

    for copy in sent:
        copy.wait_send()
    for t in order:
        sib_copies[t].wait_send()


def reduce_grads(grads, dense_grad):
    hbm = pl.BlockSpec(memory_space=pl.ANY)
    vmem = pl.BlockSpec(memory_space=pltpu.VMEM)
    dma = pltpu.SemaphoreType.DMA
    sizes = [(rows, cols) for rows, cols, _ in KINDS]

    def each(*lead):
        return [pltpu.VMEM((*lead, rows, cols), BF16) for rows, cols in sizes]

    def dense(*lead):
        return [pltpu.VMEM((*lead, 48, WIDTH), BF16)]

    return pl.pallas_call(
        reduce_kernel,
        out_shape=[jax.ShapeDtypeStruct((4, rows, cols), BF16) for rows, cols in sizes]
        + [jax.ShapeDtypeStruct((48, WIDTH), BF16)],
        in_specs=[hbm] * 5,
        out_specs=[vmem] * 5,
        scratch_shapes=each(4, 4)
        + dense(4)
        + each(4, 4)
        + dense(4)
        + each(3, 4)
        + dense(3)
        + each(4)
        + each(3)
        + dense(3)
        + each(4)
        + dense()
        + [dma((5,)), dma((5,)), dma((5,)), dma((5, 3)), dma((5, 3)), dma((5, 3)), dma((5, 3)), dma((5, 3)), dma((5, 3))],
        compiler_params=pltpu.CompilerParams(
            collective_id=3, has_side_effects=True, vmem_limit_bytes=60 * MIB
        ),
        name="reduce_grads",
    )(*grads, dense_grad)


def angle_tables():
    lane = np.arange(128) % HD
    frequency = np.exp(-math.log(10000.0) * (2.0 / ROT) * np.arange(ROT // 2)).astype(np.float32)
    tables = []
    for offset in (0, 1):
        spots = (2 * np.arange(LEN) + offset).astype(np.float32)
        angle = (spots[:, None] * frequency[None, :])[:, lane % 8].astype(np.float64)
        cosine = np.where(lane < ROT, np.cos(angle), 1.0)
        low_sine = np.where(lane < 8, -np.sin(angle), 0.0)
        high_sine = np.where((lane >= 8) & (lane < ROT), np.sin(angle), 0.0)
        tables += [cosine, low_sine, high_sine]
    return np.stack(tables).astype(np.float32)


def on_device(
    tokens_in, cotangent, positions, first_gain, first_bias, second_gain, second_bias,
    qkv_weight, qkv_bias, dense_weight, dense_bias, expand_weight, expand_bias,
    shrink_weight, shrink_bias,
):
    micro = lax.axis_index("section")
    y = lax.axis_index("seq")
    tokens = lax.dynamic_index_in_dim(tokens_in, micro, 0, keepdims=False)[0]
    cot = lax.dynamic_index_in_dim(cotangent, micro, 0, keepdims=False)[0]
    spots = lax.dynamic_index_in_dim(positions, micro, 0, keepdims=False)[0]
    spots = jnp.broadcast_to(spots[:, None], (TOK, 128))

    joint = lax.dynamic_index_in_dim(qkv_weight.reshape(48, 3, 4, GROUP), y, 2, keepdims=False)
    joint = joint.reshape(48, 3 * GROUP)
    expand = lax.dynamic_index_in_dim(expand_weight.reshape(48, 16, 4, 48), y, 2, keepdims=False)
    expand = expand.reshape(48, WIDTH)
    shrink = lax.dynamic_slice(shrink_weight[0], (48 * y, 0), (48, WIDTH))
    hidden_bias = lax.dynamic_slice(expand_bias, (0, 48 * y), (1, 48))
    vector = jnp.concatenate(
        [first_gain, first_bias, second_gain, second_bias, dense_bias, shrink_bias, hidden_bias]
        + [qkv_bias.reshape(3, 48), jnp.zeros((6, 48), BF16)],
        axis=0,
    )
    vector = jnp.pad(vector, ((0, 0), (0, 80)))

    *wholes, dense_whole = gather_weights((joint, expand, shrink, vector), dense_weight[0])
    layer_out, input_grad, *grads = run_layers(
        tokens, cot, spots, jnp.asarray(angle_tables()), wholes, dense_whole
    )
    shaped = [
        grad.reshape(2, 4, 4, rows, cols) for grad, (rows, cols, _) in zip(grads[:4], KINDS)
    ]
    joint, expand, shrink, vector, dense = reduce_grads(shaped, grads[4].reshape(2, 4, 48, WIDTH))

    joint = joint.reshape(4, 48, 3, GROUP).transpose(1, 2, 0, 3).reshape(1, 48, 3 * WIDTH)
    expand = expand.reshape(4, 48, 16, 48).transpose(1, 2, 0, 3).reshape(1, 48, 4 * WIDTH)
    shrink = shrink.reshape(1, GROUP, WIDTH)
    vector = vector[:, :, :48].astype(F32)
    summed = jnp.sum(vector, axis=0)
    hidden_bias = vector[:, 6].reshape(1, GROUP)
    shape = (1, 2, 1, TOK, WIDTH)
    return (
        layer_out.reshape(shape),
        input_grad.reshape(shape),
        summed[0:1],
        summed[1:2],
        summed[2:3],
        summed[3:4],
        joint.astype(F32),
        summed[7:10].reshape(1, 144),
        dense[None].astype(F32),
        summed[4:5],
        expand.astype(F32),
        hidden_bias,
        shrink.astype(F32),
        summed[4:5],
    )


def solution(mesh):
    tokens = P(None, "fsdp", "seq", None)
    flat = P("section", "fsdp")
    wide = P("section", "fsdp", None)
    out = P("section", None, "fsdp", "seq", None)
    return jax.shard_map(
        on_device,
        mesh=mesh,
        in_specs=(
            tokens, tokens, P(None, "fsdp", "seq"), flat, flat, flat, flat,
            wide, flat, wide, flat, wide, flat, wide, flat,
        ),
        out_specs=(
            out, out, flat, flat, flat, flat, wide, flat, wide, flat, wide, flat, wide, flat,
        ),
        check_vma=False,
    )
```

time: 1000 us -> 196 us (0.20)
  waiting for transfers between devices: 333 us -> 0 us
  Pallas kernels: 0 us -> 165 us
  local copies, waits for them, and re-layouts: 185 us -> 24.3 us
  blocking collectives: 159 us -> 0 us
  matrix products: 139 us -> 0 us
  other arithmetic: 93.2 us -> 4.61 us
  starting transfers between devices: 60.7 us -> 0 us
  between operations: 20.1 us -> 0.78 us
    reduce_scatter x4 -> x0, waiting for transfers between devices: 203 us -> none  [the longest x1 81.1 us: on_device(): lax.psum_scatter(lifted[8].astype(jnp.bfloat16), 'fsdp', scatter_dimensio...]
    pallas_call x0 -> x3, Pallas kernels: none -> 165 us  [the longest x1 78.9 us: run_layers(): pl.pallas_call(layers_kernel, out_shape=[jax.ShapeDtypeStruct(shape, BF16...]
    unnamed x2 -> x0, blocking collectives: 149 us -> none
    dot_general x57 -> x0, matrix products: 139 us -> none  [the longest x12 45.1 us: contract_rows(): lax.dot_general(left_side, right_side, (((0,), (0,)), ((), ())), preferre...]
    all_gather x4 -> x0, waiting for transfers between devices: 65.5 us -> none  [the longest x1 51.5 us: on_device(): lax.all_gather(shrink_weight, 'fsdp', axis=1, tiled=True)]
    all_to_all x12 -> x0, starting transfers between devices: 53.8 us -> none  [the longest x3 14.5 us: layer_backward(): lax.all_to_all(joined_heads_grad, 'seq', split_axis=0, concat_axis=2, til...]
    slice x39 -> x3, local copies, waits for them, and re-layouts: 43.2 us -> 0.56 us  [the longest x1 0.53 us: on_device(): summed[4:5]]
    all_to_all x33 -> x0, local copies, waits for them, and re-layouts: 34.7 us -> none  [the longest x12 13.9 us: layer_forward(): lax.all_to_all(context_heads, 'seq', split_axis=0, concat_axis=1, tiled=T...]
  transfers between devices with their start and end apart: 26 -> 0, of which waited for: 13 -> 0; matrix products, arithmetic and copies ran while one was open for 22% -> 0% of each run, Pallas kernels for 0% -> 0%
where the time goes in v1:
time: 196 us; the launch traced here: 195 us
  Pallas kernels  165 us (84%)
  local copies, waits for them, and re-layouts  24.3 us (12%)
  other arithmetic  4.61 us (2%)
    pallas_call x1, Pallas kernels, run_layers(): pl.pallas_call(layers_kernel, out_shape=[jax.ShapeDtypeStruct(shape, BF16...  78.9 us
    pallas_call x1, Pallas kernels, reduce_grads(): pl.pallas_call(reduce_kernel, out_shape=[jax.ShapeDtypeStruct((4, rows, c...  47.4 us
    pallas_call x1, Pallas kernels, gather_weights(): pl.pallas_call(gather_kernel, out_shape=[jax.ShapeDtypeStruct((2, 16 * ro...  39 us
    convert_element_type x3, local copies, waits for them, and re-layouts, on_device(): expand.astype(F32)  4.52 us

profile of v1, /device:TPU:0, one launch (start us, length us, event | category | flops | bytes accessed | tf_op | source)
XLA Modules:
  0.0 195.0 jit_solution(9194637263370979366)
XLA Ops:
  0.7 0.7 fusion.1
  1.4 0.7 reduce
  2.2 0.8 constant_dynamic-slice_fusion
  2.9 0.9 concatenate.3
  4.4 0.7 broadcast_in_dim.12.pos_ref
  5.7 1.6 dynamic-slice_bitcast_fusion
  7.3 1.2 reshape.127
  9.1 0.7 reshape.128.refs_0_
  9.8 1.7 reshape.129
  11.5 1.3 dynamic-slice_reduce_fusion
  12.8 0.8 reshape.130.refs_1_
  13.7 39.0 %gather_weights.1 = (bf16[2,768,576]{2,1,0:T(8,128)(2,1)}, bf16[2,768,768]{2,1,0:T(8,128)(2,1)}, bf16[2,768,768]{2,1,0:T(8,128)(2,1)}, bf16[2,256,128]{2,1,0:T(8,128)(2,1)}, bf16[2,192,768]{2,1,0:T(8,128)(2,1)}) custom-call(bf16[48,576]{1,0:T(8,128)(2,1)} %reshape.128.refs_0_, bf16[48,768]{1,0:T(8,128)(2,1)} %reshape.130.refs_1_, ...), custom_call_target="tpu_custom_call" | custom-call | tf_op jit(solution)/shard_map/gather_weights/pallas_call | solution.py:189
  52.7 78.9 %layers.1 = (bf16[2,64,768]{2,1,0:T(8,128)(2,1)}, bf16[2,64,768]{2,1,0:T(8,128)(2,1)}, bf16[2,768,576]{2,1,0:T(8,128)(2,1)}, bf16[2,768,768]{2,1,0:T(8,128)(2,1)...) custom-call(bf16[64,768]{1,0:T(8,128)(2,1)} %get-tuple-element.96.x_ref, ...), custom_call_target="tpu_custom_call" | custom-call | tf_op jit(solution)/shard_map/layers/pallas_call | solution.py:446
  131.7 47.4 %reduce_grads.1 = (bf16[4,48,576]{2,1,0:T(8,128)(2,1)}, bf16[4,48,768]{2,1,0:T(8,128)(2,1)}, bf16[4,48,768]{2,1,0:T(8,128)(2,1)}, bf16[4,16,128]{2,1,0:T(8,128)(2,1)}, bf16[48,768]{1,0:T(8,128)(2,1)}) custom-call(bf16[2,4,4,48,576]{4,3,2,1,0:T(8,128)(2,1)} %bitcast.33, bf16[2,4,4,48,768]{4,3,2,1,0:T(8,128)(2,1)} %bitcast.31, ...), custom_call_target="tpu_custom_call" | custom-call | tf_op jit(solution)/shard_map/reduce_grads/pallas_call | solution.py:662
  179.1 0.8 fusion
  181.1 0.7 slice_convert_fusion
  182.4 1.6 bitcast_convert_fusion.1
  184.0 1.3 reshape.144
  185.7 1.1 reshape.140
  186.8 0.9 bitcast_convert_fusion
  187.7 0.9 reshape.145
  188.5 1.0 copy.44
  189.6 2.6 %reshape.142 = f32[1,48,3072]{2,1,0:T(8,128)} reshape(f32[48,16,4,48]{3,2,1,0:T(4,128)S(1)} %copy.44) | data formatting | bytes 1179648 | tf_op jit(solution)/shard_map/convert_element_type | solution.py:753
  192.7 1.6 copy.53
  (23 shorter events, 5.3 us)
Async XLA Ops:
  0.6 4.4 %copy-start = (bf16[1,192,768]{2,1,0:T(8,128)(2,1)S(1)}, bf16[1,192,768]{2,1,0:T(8,128)(2,1)}, u32[]{:S(2)}) copy-start(bf16[1,192,768]{2,1,0:T(8,128)(2,1)} %param.29) | copy-start | bytes 884740
  179.1 7.8 %copy-start.2 = (bf16[4,48,768]{2,1,0:T(8,128)(2,1)S(1)}, bf16[4,48,768]{2,1,0:T(8,128)(2,1)}, u32[]{:S(2)}) copy-start(bf16[4,48,768]{2,1,0:T(8,128)(2,1)} %get-tuple-element.47) | copy-start | bytes 884740
  179.1 8.6 %copy-start.1 = (bf16[4,48,768]{2,1,0:T(8,128)(2,1)S(1)}, bf16[4,48,768]{2,1,0:T(8,128)(2,1)}, u32[]{:S(2)}) copy-start(bf16[4,48,768]{2,1,0:T(8,128)(2,1)} %get-tuple-element.46) | copy-start | bytes 884740
  180.4 11.8 %copy-start.4 = (f32[1,48]{1,0:T(1,128)}, f32[1,48]{1,0:T(1,128)S(1)}, u32[]{:S(2)}) copy-start(f32[1,48]{1,0:T(1,128)S(1)} %get-tuple-element.148) | copy-start | bytes 580
  189.6 4.8 %copy-start.3 = (bf16[2,64,768]{2,1,0:T(8,128)(2,1)S(1)}, bf16[2,64,768]{2,1,0:T(8,128)(2,1)}, u32[]{:S(2)}) copy-start(bf16[2,64,768]{2,1,0:T(8,128)(2,1)} %get-tuple-element.37) | copy-start | bytes 589828

commit v2 on v1

v2 whole, which is shorter than its diff:
```python
import math

import jax
import jax.numpy as jnp
import numpy as np
from jax import lax
from jax.experimental import pallas as pl
from jax.experimental.pallas import tpu as pltpu
from jax.sharding import PartitionSpec as P

MESH = pl.DeviceIdType.MESH
F32 = jnp.float32
BF16 = jnp.bfloat16
HD = 64
ROT = 16
WIDTH = 768
TOK = 64
LEN = 256
GROUP = 192
NEAR = (1, 3, 2)
MIB = 1024 * 1024

KINDS = ((48, 576, False), (48, 768, True), (48, 768, False), (16, 128, True))


def ring(value, by):
    return lax.rem(value + by, 4)


def places():
    owner = lax.axis_index("fsdp")
    return owner, lax.div(owner, 4), lax.rem(owner, 4)


def joined(u, v, x_first):
    return u * 4 + v if x_first else v * 4 + u


def remote(src, dst, send, recv, target):
    return pltpu.make_async_remote_copy(
        src_ref=src, dst_ref=dst, send_sem=send, recv_sem=recv, device_id=target, device_id_type=MESH
    )


def greet(targets):
    barrier = pltpu.get_barrier_semaphore()
    for target in targets:
        pl.semaphore_signal(barrier, inc=1, device_id=target, device_id_type=MESH)
    pl.semaphore_wait(barrier, len(targets))


def sheet_peers(x, z):
    return [{"fsdp": ring(x, d) * 4 + z} for d in (1, 2, 3)] + [
        {"fsdp": x * 4 + ring(z, d)} for d in (1, 2, 3)
    ]


def seq_peers(y):
    return [{"seq": ring(y, d)} for d in (1, 2, 3)]


def dot(a, b):
    return jnp.dot(a, b, preferred_element_type=F32)


def dot_nt(a, b):
    return lax.dot_general(a, b, (((1,), (1,)), ((), ())), preferred_element_type=F32)


def dot_tn(a, b):
    return lax.dot_general(a, b, (((0,), (0,)), ((), ())), preferred_element_type=F32)


def turn_tables(tab_ref, odd, sign):
    tables = []
    for i in range(3):
        table = jnp.where(odd, tab_ref[3 + i], tab_ref[i])
        if i and sign < 0:
            table = -table
        tables.append(jnp.concatenate([table] * 3, axis=1))
    return tables


def turn(values, tables):
    cosine, low_sine, high_sine = tables
    span = values.shape[1]
    return (
        values * cosine
        + pltpu.roll(values, span - 8, 1) * low_sine
        + pltpu.roll(values, 8, 1) * high_sine
    )


def column_block(shape):
    col = lax.broadcasted_iota(jnp.int32, shape, 1)
    return lax.shift_right_logical(col * 43691, 21)


def piece_mask(shape):
    row = lax.broadcasted_iota(jnp.int32, shape, 0)
    return lax.shift_right_logical(row, 4) == column_block(shape)


def joint_mask(shape, y):
    row = lax.broadcasted_iota(jnp.int32, shape, 0)
    k = (row & 15) - 7
    chunk = 3 * lax.shift_right_logical(row, 4) + k
    block = column_block(shape)
    wanted = 16 * lax.shift_right_logical(block, 2) + (block & 3) + 4 * y
    return (k >= 0) & (k < 3) & (chunk == wanted)


def spread_matrix():
    shape = (128, WIDTH)
    col = lax.broadcasted_iota(jnp.int32, shape, 1)
    row = lax.broadcasted_iota(jnp.int32, shape, 0)
    return jnp.where(col - 48 * column_block(shape) == row, 1.0, 0.0).astype(BF16)

ORDER = (0, 3, 1, 2)
BACK = (2, 1, 4, 0, 3)


def program_kernel(*refs):
    (
        x_ref, cot_ref, pos_ref, tab_ref, fg, fb, sg, sb, db, hb, qb, eb, qw, ew, sw, dw,
        out_q, out_e, out_s, out_v, out_d, lo_out, ig_out,
        qs, es, vs, vecf, wq, we, ws, wv, wd,
        dq, de, ds, dv, dd, hq, he, hs, hv, hd, aq, ae, as_, av, ad,
        mq, me, ms, mv, md, nq, ne, ns, nv, nd,
        xall, dyall, posall, part, psend, prec, qkvs, probs, ctx, acts, slopes,
        n1s, n2s, xhs, vrows, bqs, grows, staged,
        gsend, grecv, dsend, drecv, csend, crecv,
        asend, arecv, rsend, rrecv, posend, porecv,
        hsend, hrecv, wsend, wrecv, bsend, brecv, ysend, yrecv, osend, orecv,
    ) = refs
    micro = lax.axis_index("section")
    y = lax.axis_index("seq")
    owner, x, z = places()
    sibling = {"section": 1 - micro}
    holds = x == y
    own = pl.ds(pl.multiple_of(y * TOK, TOK), TOK)

    peers = sheet_peers(x, z) + seq_peers(y) + [sibling]
    barrier = pltpu.get_barrier_semaphore()
    for target in peers:
        pl.semaphore_signal(barrier, inc=1, device_id=target, device_id_type=MESH)

    vecf[...] = jnp.zeros_like(vecf)
    for i, ref in enumerate((fg, fb, sg, sb, db, hb)):
        vecf[i : i + 1, 0:48] = ref[...].astype(F32)
    for k in range(3):
        vecf[7 + k : 8 + k, 0:48] = qb[:, 48 * k : 48 * k + 48].astype(F32)
    for h in range(4):

        @pl.when(y == h)
        def _():
            qs[...] = jnp.concatenate(
                [qw[0, :, WIDTH * t + GROUP * h : WIDTH * t + GROUP * (h + 1)] for t in range(3)], axis=1
            )
            es[...] = jnp.concatenate(
                [ew[0, :, GROUP * f + 48 * h : GROUP * f + 48 * h + 48] for f in range(16)], axis=1
            )
            vecf[6:7, 0:48] = eb[:, 48 * h : 48 * h + 48].astype(F32)

    vs[...] = vecf[...].astype(BF16)
    shrink_rows = sw.at[0, pl.ds(pl.multiple_of(48 * y, 16), 48), :]
    shards = (qs, es, shrink_rows, vs)
    wholes = (wq, we, ws, wv, wd)

    def slot(t, l, s):
        rows = KINDS[t][0]
        return wholes[t].at[l, pl.ds(pl.multiple_of(s * rows, 16), rows), :]

    def band(l, i):
        return wd.at[l, pl.ds(pl.multiple_of(i * 48, 16), 48), :]

    def mine(rows):
        return pl.ds(pl.multiple_of(owner * rows, 16), rows)

    wq[micro, mine(48), :] = qs[...]
    we[micro, mine(48), :] = es[...]
    ws[micro, mine(48), :] = shrink_rows[...]
    wv[micro, mine(16), :] = vs[...]
    dense_mine = pl.ds(pl.multiple_of(z * 48, 16), 48)

    @pl.when(holds)
    def _():
        wd[micro, dense_mine, :] = dw[0]

    xall[0, own, :] = x_ref[micro, 0]
    dyall[1, own, :] = cot_ref[micro, 0]
    shape = (TOK, TOK)
    level = lax.broadcasted_iota(jnp.int32, shape, 0) == lax.broadcasted_iota(jnp.int32, shape, 1)
    spots = jnp.where(level, jnp.broadcast_to(pos_ref[micro].astype(F32), shape), 0.0)
    posall[own, :] = jnp.broadcast_to(jnp.sum(spots, axis=1, keepdims=True), (TOK, 128))
    pl.semaphore_wait(barrier, len(peers))

    def axes(t):
        x_first = KINDS[t][2]
        return (x, z, x_first) if x_first else (z, x, x_first)

    def gather_start(l):
        for t in ORDER:
            u, v, x_first = axes(t)
            for k, d in enumerate(NEAR):
                remote(
                    shards[t], slot(t, l, owner), gsend.at[t, k], grecv.at[t, owner],
                    {"fsdp": joined(ring(u, d), v, x_first)},
                ).start()

        @pl.when(holds)
        def _():
            for k, d in enumerate(NEAR):
                remote(
                    dw.at[0], band(l, z), dsend.at[k], drecv.at[z], {"fsdp": ring(x, d) * 4 + z}
                ).start()

    def gather_forward(l):
        for t in ORDER:
            u, v, x_first = axes(t)
            for d in (0, 1, 3, 2):
                s = joined(ring(u, 4 - d), v, x_first)
                if d:
                    remote(slot(t, l, s), slot(t, l, s), gsend.at[t, 0], grecv.at[t, s], sibling).wait_recv()
                for k, e in enumerate(NEAR):
                    remote(
                        slot(t, l, s), slot(t, l, s), gsend.at[t, 3 + 3 * d + k], grecv.at[t, s],
                        {"fsdp": joined(u, ring(v, e), x_first)},
                    ).start()

        @pl.when(jnp.logical_not(holds))
        def _():
            remote(band(l, z), band(l, z), dsend.at[0], drecv.at[z], sibling).wait_recv()

        for k, e in enumerate(NEAR):
            remote(
                band(l, z), band(l, z), dsend.at[3 + k], drecv.at[z], {"fsdp": x * 4 + ring(z, e)}
            ).start()

    def need(t, l):
        @pl.when(micro == l)
        def _():
            if t < 4:
                u, v, x_first = axes(t)
                for e in NEAR:
                    for d in (0, 1, 3, 2):
                        s = joined(ring(u, 4 - d), ring(v, 4 - e), x_first)
                        remote(slot(t, l, s), slot(t, l, s), gsend.at[t, 0], grecv.at[t, s], sibling).wait_recv()
            else:
                for e in NEAR:
                    i = ring(z, 4 - e)
                    remote(band(l, i), band(l, i), dsend.at[0], drecv.at[i], sibling).wait_recv()
            remote(wholes[t].at[l], wholes[t].at[l], csend.at[t], crecv.at[t], sibling).start()

        @pl.when(micro != l)
        def _():
            remote(wholes[t].at[l], wholes[t].at[l], csend.at[t], crecv.at[t], sibling).wait_recv()

    def rows_of(i):
        return pl.ds(pl.multiple_of(i * TOK, TOK), TOK)

    def share(ref, sends, recvs):
        for k, d in enumerate(NEAR):
            remote(ref.at[own, :], ref.at[own, :], sends.at[k], recvs.at[k], {"seq": ring(y, d)}).start()

    def collect(ref, sends, recvs):
        for k, d in enumerate(NEAR):
            src = ref.at[rows_of(ring(y, 4 - d)), :]
            remote(src, src, sends.at[k], recvs.at[k], sibling).wait_recv()

    def reduce_start(value, back, l):
        part[back, l] = value
        psend[back, l] = value.astype(BF16)
        for k, d in enumerate(NEAR):
            to = ring(y, d)
            remote(
                psend.at[back, l, rows_of(to), :], prec.at[back, l, k],
                rsend.at[back, l, k], rrecv.at[back, l, k], {"seq": to},
            ).start()

    def reduce_end(back, l):
        total = part[back, l, own, :]
        for k in range(3):
            remote(
                prec.at[back, l, k], prec.at[back, l, k],
                rsend.at[back, l, k], rrecv.at[back, l, k], sibling,
            ).wait_recv()
            total = total + prec[back, l, k].astype(F32)
        return total

    share(xall.at[0], asend.at[0, 0], arecv.at[0, 0])
    share(posall, posend, porecv)

    @pl.when(micro == 0)
    def _():
        gather_start(0)

    share(dyall.at[1], asend.at[1, 1], arecv.at[1, 1])

    @pl.when(micro == 0)
    def _():
        gather_forward(0)

    collect(posall, posend, porecv)
    token = lax.broadcasted_iota(jnp.int32, (LEN, 128), 0)
    odd = posall[...] > (2 * token).astype(F32) + 0.5

    def forward(l):
        need(3, l)
        columns = dot(wv[l], spread_matrix())
        vrows[l] = jnp.sum(
            jnp.where(piece_mask((LEN, WIDTH)), columns, 0.0).reshape(16, 16, WIDTH), axis=0
        )
        bqs[l] = jnp.broadcast_to(
            jnp.sum(
                jnp.where(joint_mask((LEN, 3 * GROUP), y), columns[:, : 3 * GROUP], 0.0),
                axis=0,
                keepdims=True,
            ),
            (8, 3 * GROUP),
        )
        collect(xall.at[l], asend.at[0, l], arecv.at[0, l])
        values = xall[l].astype(F32)
        center = values - jnp.mean(values, axis=-1, keepdims=True)
        scale = lax.rsqrt(jnp.mean(center * center, axis=-1, keepdims=True) + 1e-5)
        normed = center * scale
        xhs[l] = normed
        n1 = (normed * vrows[l, 0:1, :] + vrows[l, 1:2, :]).astype(BF16)
        n2 = (normed * vrows[l, 2:3, :] + vrows[l, 3:4, :]).astype(BF16)
        n1s[l] = n1
        n2s[l] = n2
        need(0, l)
        joint = dot(n1, wq[l]) + bqs[l, 0:1, :]
        turned = turn(joint[:, : 2 * GROUP], turn_tables(tab_ref, odd, 1))
        qkvs[l, :, : 2 * GROUP] = turned.astype(BF16)
        qkvs[l, :, 2 * GROUP :] = joint[:, 2 * GROUP :].astype(BF16)
        row = lax.broadcasted_iota(jnp.int32, (LEN, LEN), 0)
        allowed = row >= lax.broadcasted_iota(jnp.int32, (LEN, LEN), 1)
        for n in range(3):
            q = qkvs[l, :, n * HD : (n + 1) * HD]
            k = qkvs[l, :, GROUP + n * HD : GROUP + (n + 1) * HD]
            v = qkvs[l, :, 2 * GROUP + n * HD : 2 * GROUP + (n + 1) * HD]
            scores = jnp.where(allowed, dot_nt(q, k) * HD**-0.5, -1e30)
            powers = jnp.exp(scores - jnp.max(scores, axis=-1, keepdims=True))
            prob = powers / jnp.sum(powers, axis=-1, keepdims=True)
            probs[l, n] = prob
            ctx[l, :, n * HD : (n + 1) * HD] = dot(prob.astype(BF16), v).astype(BF16)
        if l == 0:

            @pl.when(micro == 1)
            def _():
                gather_start(1)

        need(1, l)
        hidden = dot(n2, we[l]) + vrows[l, 6:7, :]
        phi = 0.5 + 0.5 * lax.erf(hidden * math.sqrt(0.5))
        acts[l] = (hidden * phi).astype(BF16)
        if l == 0:

            @pl.when(micro == 1)
            def _():
                gather_forward(1)

        need(4, l)
        need(2, l)
        reduce_start(dot(ctx[l], wd[l]) + dot(acts[l], ws[l]), 0, l)
        density = jnp.exp(-0.5 * hidden * hidden) * (1.0 / math.sqrt(2.0 * math.pi))
        slopes[l] = phi + hidden * density

    def forward_end(l):
        total = reduce_end(0, l)
        result = xall[l, own, :].astype(F32) + total + vrows[l, 4:5, :] + vrows[l, 5:6, :]
        return result.astype(BF16)

    grads = (dq, de, ds, dv, dd)
    helds = (hq, he, hs, hv, hd)
    wides = (aq, ae, as_, av, ad)
    mids = (mq, me, ms, mv, md)
    narrows = (nq, ne, ns, nv, nd)
    outs = (out_q, out_e, out_s, out_v, out_d)

    def keep(t, l, value):
        rows = KINDS[t][0] if t < 4 else 48
        value = value.astype(BF16)
        for b in range(value.shape[0] // rows):
            piece = value[b * rows : (b + 1) * rows]
            if t < 4:
                grads[t][l, b // 4, b % 4] = piece
            else:
                grads[t][l, b] = piece

        @pl.when(micro != l)
        def _():
            remote(grads[t].at[l], helds[t], hsend.at[t], hrecv.at[t], sibling).start()

    def fold(t, l):
        remote(helds[t], helds[t], hsend.at[t], hrecv.at[t], sibling).wait_recv()
        grad, held = grads[t], helds[t]
        if t == 4:
            for i in range(4):
                grad[l, i] = (grad[l, i].astype(F32) + held[i].astype(F32)).astype(BF16)
            for k, e in enumerate(NEAR):
                to = ring(z, e)
                remote(
                    grad.at[l, to], wides[t].at[k], wsend.at[t, k], wrecv.at[t, k], {"fsdp": x * 4 + to}
                ).start()
            return

        def add(i, carry):
            a, b = lax.div(i, 4), lax.rem(i, 4)
            grad[l, a, b] = (grad[l, a, b].astype(F32) + held[a, b].astype(F32)).astype(BF16)
            return carry

        lax.fori_loop(0, 16, add, 0)
        u, v, x_first = axes(t)
        for k, e in enumerate(NEAR):
            to = ring(v, e)
            remote(
                grad.at[l, :, to] if x_first else grad.at[l, to],
                wides[t].at[k], wsend.at[t, k], wrecv.at[t, k], {"fsdp": joined(u, to, x_first)},
            ).start()

    def wide_end(t, l):
        grad = grads[t]
        for k in range(3):
            remote(wides[t].at[k], wides[t].at[k], wsend.at[t, k], wrecv.at[t, k], sibling).wait_recv()
        if t == 4:
            total = grad[l, z].astype(F32)
            for k in range(3):
                total = total + wides[t][k].astype(F32)
            mids[t][...] = total.astype(BF16)

            @pl.when(jnp.logical_not(holds))
            def _():
                away = ring(x, 4 - y) - 1
                remote(
                    mids[t], narrows[t].at[away], bsend.at[t, 0], brecv.at[t, away], {"fsdp": y * 4 + z}
                ).start()

            return
        u, v, x_first = axes(t)
        for d in (1, 3, 2, 0):
            to = ring(u, d)
            total = grad[l, to, v].astype(F32) if x_first else grad[l, v, to].astype(F32)
            for k in range(3):
                total = total + wides[t][k, to].astype(F32)
            mids[t][to] = total.astype(BF16)
            if d:
                k = NEAR.index(d)
                remote(
                    mids[t].at[to], narrows[t].at[k], bsend.at[t, k], brecv.at[t, k],
                    {"fsdp": joined(to, v, x_first)},
                ).start()

    def narrow_end(t):
        if t == 4:

            @pl.when(holds)
            def _():
                total = mids[t][...].astype(F32)
                for k in range(3):
                    remote(narrows[t].at[k], narrows[t].at[k], bsend.at[t, 0], brecv.at[t, k], sibling).wait_recv()
                    total = total + narrows[t][k].astype(F32)
                out_d[...] = total.astype(BF16)
                for k, d in enumerate(NEAR):
                    remote(out_d, out_d, ysend.at[t, k], yrecv.at[t, 0], {"seq": ring(y, d)}).start()

            return
        u, v, x_first = axes(t)
        total = mids[t][u].astype(F32)
        for k in range(3):
            remote(narrows[t].at[k], narrows[t].at[k], bsend.at[t, k], brecv.at[t, k], sibling).wait_recv()
            total = total + narrows[t][k].astype(F32)
        outs[t][y] = total.astype(BF16)
        for k, d in enumerate(NEAR):
            remote(
                outs[t].at[y], outs[t].at[y], ysend.at[t, k], yrecv.at[t, k], {"seq": ring(y, d)}
            ).start()

    def hidden_back(l):
        out_grad = dyall[l]
        return (dot_nt(out_grad, ws[l]) * slopes[l]).astype(BF16)

    def hidden_weights(l, hidden_grad):
        out_grad = dyall[l]
        keep(2, l, dot_tn(acts[l], out_grad))
        keep(1, l, dot_tn(n2s[l], hidden_grad))
        keep(4, l, dot_tn(ctx[l], out_grad))

    def attention_back(l):
        ctx_grad = dot_nt(dyall[l], wd[l]).astype(BF16)
        parts = ([], [], [])
        for n in range(3):
            q = qkvs[l, :, n * HD : (n + 1) * HD]
            k = qkvs[l, :, GROUP + n * HD : GROUP + (n + 1) * HD]
            v = qkvs[l, :, 2 * GROUP + n * HD : 2 * GROUP + (n + 1) * HD]
            up = ctx_grad[:, n * HD : (n + 1) * HD]
            prob = probs[l, n]
            prob_grad = dot_nt(up, v)
            inner = jnp.sum(prob * prob_grad, axis=-1, keepdims=True)
            score_grad = (prob * (prob_grad - inner)).astype(BF16)
            parts[0].append(dot(score_grad, k) * HD**-0.5)
            parts[1].append(dot_tn(score_grad, q) * HD**-0.5)
            parts[2].append(dot_tn(prob.astype(BF16), up))
        turned_grad = jnp.concatenate(parts[0] + parts[1], axis=1).astype(BF16).astype(F32)
        return jnp.concatenate(
            [turn(turned_grad, turn_tables(tab_ref, odd, -1))] + parts[2], axis=1
        ).astype(BF16)

    def vector_grads(l, hidden_grad, joint_grad, n1_grad, n2_grad):
        normed = xhs[l]
        grows[...] = jnp.zeros_like(grows)
        grows[0:1, :] = jnp.sum(n1_grad * normed, axis=0, keepdims=True)
        grows[1:2, :] = jnp.sum(n1_grad, axis=0, keepdims=True)
        grows[2:3, :] = jnp.sum(n2_grad * normed, axis=0, keepdims=True)
        grows[3:4, :] = jnp.sum(n2_grad, axis=0, keepdims=True)
        grows[4:5, :] = jnp.sum(dyall[l, own, :].astype(F32), axis=0, keepdims=True)
        grows[6:7, :] = jnp.sum(hidden_grad.astype(F32), axis=0, keepdims=True)
        joint_bias = jnp.sum(joint_grad.astype(F32), axis=0, keepdims=True)
        spread = spread_matrix()
        first = jnp.where(piece_mask((LEN, WIDTH)), jnp.concatenate([grows[...]] * 16, axis=0), 0.0)
        second = jnp.where(
            joint_mask((LEN, 3 * GROUP), y), jnp.broadcast_to(joint_bias, (LEN, 3 * GROUP)), 0.0
        )
        keep(
            3,
            l,
            dot_nt(first.astype(BF16), spread) + dot_nt(second.astype(BF16), spread[:, : 3 * GROUP]),
        )

    def backward_end(l):
        total = reduce_end(1, l)
        values = xall[l, own, :].astype(F32)
        center = values - jnp.mean(values, axis=-1, keepdims=True)
        scale = lax.rsqrt(jnp.mean(center * center, axis=-1, keepdims=True) + 1e-5)
        near = center * scale
        pulled = scale * (
            total
            - jnp.mean(total, axis=-1, keepdims=True)
            - near * jnp.mean(total * near, axis=-1, keepdims=True)
        )
        return (dyall[l, own, :].astype(F32) + pulled).astype(BF16)

    forward(0)
    middle = forward_end(0)
    xall[1, own, :] = middle
    share(xall.at[1], asend.at[0, 1], arecv.at[0, 1])
    staged[0, 0] = middle
    forward(1)

    collect(dyall.at[1], asend.at[1, 1], arecv.at[1, 1])
    hidden_grad = hidden_back(1)
    n2_grad = dot_nt(hidden_grad, we[1])
    joint_grad = attention_back(1)
    n1_grad = dot_nt(joint_grad, wq[1])
    reduce_start(n1_grad * vrows[1, 0:1, :] + n2_grad * vrows[1, 2:3, :], 1, 1)
    hidden_weights(1, hidden_grad)
    keep(0, 1, dot_tn(n1s[1], joint_grad))
    vector_grads(1, hidden_grad, joint_grad, n1_grad, n2_grad)
    staged[0, 1] = forward_end(1)
    upper = backward_end(1)
    dyall[0, own, :] = upper
    share(dyall.at[0], asend.at[1, 0], arecv.at[1, 0])
    staged[1, 1] = upper
    remote(staged.at[0, 1 - micro], lo_out.at[micro], osend.at[0], orecv.at[0], sibling).start()

    @pl.when(micro == 1)
    def _():
        for t in BACK:
            fold(t, 1)

    collect(dyall.at[0], asend.at[1, 0], arecv.at[1, 0])
    hidden_grad = hidden_back(0)
    hidden_weights(0, hidden_grad)
    joint_grad = attention_back(0)
    keep(0, 0, dot_tn(n1s[0], joint_grad))
    n1_grad = dot_nt(joint_grad, wq[0])
    n2_grad = dot_nt(hidden_grad, we[0])
    reduce_start(n1_grad * vrows[0, 0:1, :] + n2_grad * vrows[0, 2:3, :], 1, 0)
    vector_grads(0, hidden_grad, joint_grad, n1_grad, n2_grad)

    @pl.when(micro == 0)
    def _():
        for t in BACK:
            fold(t, 0)

    @pl.when(micro == 1)
    def _():
        for t in BACK:
            wide_end(t, 1)

    staged[1, 0] = backward_end(0)
    remote(staged.at[1, 1 - micro], ig_out.at[micro], osend.at[1], orecv.at[1], sibling).start()
    lo_out[micro] = staged[0, micro]
    ig_out[micro] = staged[1, micro]

    @pl.when(micro == 0)
    def _():
        for t in BACK:
            wide_end(t, 0)

    for t in BACK:
        narrow_end(t)

    for t in range(4):
        for k, d in enumerate(NEAR):
            src = outs[t].at[ring(y, 4 - d)]
            remote(src, src, ysend.at[t, k], yrecv.at[t, k], sibling).wait_recv()
            remote(src, src, ysend.at[t, k], yrecv.at[t, k], sibling).wait_send()
            remote(narrows[t].at[k], narrows[t].at[k], bsend.at[t, k], brecv.at[t, k], sibling).wait_send()
        for k in range(15):
            remote(shards[t], shards[t], gsend.at[t, k], grecv.at[t, 0], sibling).wait_send()
    for t in range(5):
        for k in range(3):
            remote(wides[t].at[k], wides[t].at[k], wsend.at[t, k], wrecv.at[t, k], sibling).wait_send()
        remote(wholes[t].at[0], wholes[t].at[0], csend.at[t], crecv.at[t], sibling).wait_send()
        remote(helds[t], helds[t], hsend.at[t], hrecv.at[t], sibling).wait_send()

    @pl.when(holds)
    def _():
        for k in range(3):
            remote(out_d, out_d, ysend.at[4, k], yrecv.at[4, 0], sibling).wait_send()
            remote(dw.at[0], dw.at[0], dsend.at[k], drecv.at[0], sibling).wait_send()

    @pl.when(jnp.logical_not(holds))
    def _():
        remote(out_d, out_d, ysend.at[4, 0], yrecv.at[4, 0], sibling).wait_recv()
        remote(md, md, bsend.at[4, 0], brecv.at[4, 0], sibling).wait_send()

    for k in range(3):
        remote(band(0, 0), band(0, 0), dsend.at[3 + k], drecv.at[0], sibling).wait_send()
        remote(posall.at[own, :], posall.at[own, :], posend.at[k], porecv.at[k], sibling).wait_send()
        for l in range(2):
            for back in range(2):
                src = xall.at[0, own, :]
                remote(src, src, asend.at[back, l, k], arecv.at[back, l, k], sibling).wait_send()
                src = prec.at[back, l, k]
                remote(src, src, rsend.at[back, l, k], rrecv.at[back, l, k], sibling).wait_send()
    for i, ref in enumerate((lo_out, ig_out)):
        remote(ref.at[0], ref.at[0], osend.at[i], orecv.at[i], sibling).wait()


def run_program(tokens, cot, positions, tables, vectors, weights):
    vmem = pl.BlockSpec(memory_space=pltpu.VMEM)
    dma = pltpu.SemaphoreType.DMA
    sizes = [(rows, cols) for rows, cols, _ in KINDS]

    def stacks(lead, dense_lead):
        return [pltpu.VMEM((*lead, rows, cols), BF16) for rows, cols in sizes] + [
            pltpu.VMEM((*dense_lead, 48, WIDTH), BF16)
        ]

    return pl.pallas_call(
        program_kernel,
        out_shape=[jax.ShapeDtypeStruct((4, rows, cols), BF16) for rows, cols in sizes]
        + [jax.ShapeDtypeStruct((48, WIDTH), BF16)]
        + [jax.ShapeDtypeStruct((2, TOK, WIDTH), BF16)] * 2,
        in_specs=[vmem] * 16,
        out_specs=[vmem] * 7,
        scratch_shapes=[
            pltpu.VMEM((48, 3 * GROUP), BF16),
            pltpu.VMEM((48, WIDTH), BF16),
            pltpu.VMEM((16, 128), BF16),
            pltpu.VMEM((16, 128), F32),
        ]
        + [pltpu.VMEM((2, 16 * rows, cols), BF16) for rows, cols in sizes]
        + [pltpu.VMEM((2, GROUP, WIDTH), BF16)]
        + stacks((2, 4, 4), (2, 4))
        + stacks((4, 4), (4,))
        + stacks((3, 4), (3,))
        + stacks((4,), ())
        + stacks((3,), (3,))
        + [
            pltpu.VMEM((2, LEN, WIDTH), BF16),
            pltpu.VMEM((2, LEN, WIDTH), BF16),
            pltpu.VMEM((LEN, 128), F32),
            pltpu.VMEM((2, 2, LEN, WIDTH), F32),
            pltpu.VMEM((2, 2, LEN, WIDTH), BF16),
            pltpu.VMEM((2, 2, 3, TOK, WIDTH), BF16),
            pltpu.VMEM((2, LEN, 3 * GROUP), BF16),
            pltpu.VMEM((2, 3, LEN, LEN), F32),
            pltpu.VMEM((2, LEN, GROUP), BF16),
            pltpu.VMEM((2, LEN, WIDTH), BF16),
            pltpu.VMEM((2, LEN, WIDTH), F32),
            pltpu.VMEM((2, LEN, WIDTH), BF16),
            pltpu.VMEM((2, LEN, WIDTH), BF16),
            pltpu.VMEM((2, LEN, WIDTH), F32),
            pltpu.VMEM((2, 16, WIDTH), F32),
            pltpu.VMEM((2, 8, 3 * GROUP), F32),
            pltpu.VMEM((16, WIDTH), F32),
            pltpu.VMEM((2, 2, TOK, WIDTH), BF16),
            dma((4, 15)),
            dma((4, 16)),
            dma((6,)),
            dma((4,)),
            dma((5,)),
            dma((5,)),
            dma((2, 2, 3)),
            dma((2, 2, 3)),
            dma((2, 2, 3)),
            dma((2, 2, 3)),
            dma((3,)),
            dma((3,)),
            dma((5,)),
            dma((5,)),
            dma((5, 3)),
            dma((5, 3)),
            dma((5, 3)),
            dma((5, 3)),
            dma((5, 3)),
            dma((5, 3)),
            dma((2,)),
            dma((2,)),
        ],
        compiler_params=pltpu.CompilerParams(
            collective_id=1, has_side_effects=True, vmem_limit_bytes=58 * MIB
        ),
        name="layers",
    )(tokens, cot, positions, tables, *vectors, *weights)


def lay_out_kernel(
    q, e, s, v, d, lo, ig,
    lo_out, ig_out, o0, o1, o2, o3, q_out, qb_out, d_out, db_out, e_out, eb_out, s_out, sb_out,
):
    lo_out[...] = lo[...]
    ig_out[...] = ig[...]
    for t in range(3):
        for h in range(4):
            at = WIDTH * t + GROUP * h
            q_out[0, :, at : at + GROUP] = q[h, :, GROUP * t : GROUP * (t + 1)].astype(F32)
    for f in range(0, 16, 2):
        e_out[0, :, GROUP * f : GROUP * (f + 2)] = jnp.concatenate(
            [e[h, :, 48 * i : 48 * i + 48].astype(F32) for i in (f, f + 1) for h in range(4)], axis=1
        )
    for h in range(4):
        s_out[0, 48 * h : 48 * h + 48, :] = s[h].astype(F32)
    d_out[0] = d[...].astype(F32)
    total = v[0].astype(F32) + v[1].astype(F32) + v[2].astype(F32) + v[3].astype(F32)
    for i, ref in enumerate((o0, o1, o2, o3, db_out)):
        ref[...] = total[i : i + 1, 0:48]
    sb_out[...] = total[4:5, 0:48]
    qb_out[...] = jnp.concatenate([total[7 + k : 8 + k, 0:48] for k in range(3)], axis=1)
    eb_out[...] = jnp.concatenate([v[h].astype(F32)[6:7, 0:48] for h in range(4)], axis=1)


def lay_out(parts):
    vmem = pl.BlockSpec(memory_space=pltpu.VMEM)
    flat = jax.ShapeDtypeStruct((1, 48), F32)
    rows = jax.ShapeDtypeStruct((2, TOK, WIDTH), BF16)

    def wide(height, width):
        return jax.ShapeDtypeStruct((1, height, width), F32)

    shapes = [
        rows, rows, flat, flat, flat, flat, wide(48, 3 * WIDTH), jax.ShapeDtypeStruct((1, 144), F32),
        wide(48, WIDTH), flat, wide(48, 4 * WIDTH), jax.ShapeDtypeStruct((1, GROUP), F32),
        wide(GROUP, WIDTH), flat,
    ]
    return pl.pallas_call(
        lay_out_kernel,
        out_shape=shapes,
        in_specs=[vmem] * 7,
        out_specs=[vmem] * 14,
        compiler_params=pltpu.CompilerParams(vmem_limit_bytes=32 * MIB),
        name="lay_out",
    )(*parts)


def angle_tables():
    lane = np.arange(128) % HD
    frequency = np.exp(-math.log(10000.0) * (2.0 / ROT) * np.arange(ROT // 2)).astype(np.float32)
    tables = []
    for offset in (0, 1):
        spots = (2 * np.arange(LEN) + offset).astype(np.float32)
        angle = (spots[:, None] * frequency[None, :])[:, lane % 8].astype(np.float64)
        cosine = np.where(lane < ROT, np.cos(angle), 1.0)
        low_sine = np.where(lane < 8, -np.sin(angle), 0.0)
        high_sine = np.where((lane >= 8) & (lane < ROT), np.sin(angle), 0.0)
        tables += [cosine, low_sine, high_sine]
    return np.stack(tables).astype(np.float32)


def on_device(
    tokens_in, cotangent, positions, first_gain, first_bias, second_gain, second_bias,
    qkv_weight, qkv_bias, dense_weight, dense_bias, expand_weight, expand_bias,
    shrink_weight, shrink_bias,
):
    parts = run_program(
        tokens_in,
        cotangent,
        positions,
        jnp.asarray(angle_tables()),
        (first_gain, first_bias, second_gain, second_bias, dense_bias, shrink_bias, qkv_bias, expand_bias),
        (qkv_weight, expand_weight, shrink_weight, dense_weight),
    )
    layer_out, input_grad, *rest = lay_out(parts)
    shape = (1, 2, 1, TOK, WIDTH)
    return (layer_out.reshape(shape), input_grad.reshape(shape), *rest)


def solution(mesh):
    tokens = P(None, "fsdp", "seq", None)
    flat = P("section", "fsdp")
    wide = P("section", "fsdp", None)
    out = P("section", None, "fsdp", "seq", None)
    return jax.shard_map(
        on_device,
        mesh=mesh,
        in_specs=(
            tokens, tokens, P(None, "fsdp", "seq"), flat, flat, flat, flat,
            wide, flat, wide, flat, wide, flat, wide, flat,
        ),
        out_specs=(
            out, out, flat, flat, flat, flat, wide, flat, wide, flat, wide, flat, wide, flat,
        ),
        check_vma=False,
    )
```

time: 196 us -> 108 us (0.55)
  Pallas kernels: 165 us -> 99.9 us
  local copies, waits for them, and re-layouts: 24.3 us -> 6.31 us
  other arithmetic: 4.61 us -> 0 us
    pallas_call x3 -> x2, Pallas kernels: 165 us -> 99.9 us  [the longest x1 98.3 us: run_program(): pl.pallas_call(program_kernel, out_shape=[jax.ShapeDtypeStruct((4, rows,...]
    convert_element_type x6 -> x0, local copies, waits for them, and re-layouts: 7.33 us -> none  [the longest x3 4.52 us: on_device(): expand.astype(F32)]
    reshape x6 -> x0, local copies, waits for them, and re-layouts: 5.26 us -> none  [the longest x1 1.72 us: on_device(): expand_weight.reshape(48, 16, 4, 48)]
    unnamed x13 -> x14, local copies, waits for them, and re-layouts: 2.83 us -> 6.31 us
    dynamic_slice x4 -> x0, local copies, waits for them, and re-layouts: 3.19 us -> none  [the longest x1 1.3 us: on_device(): lax.dynamic_index_in_dim(expand_weight.reshape(48, 16, 4, 48), y, 2, keep...]
    convert_element_type x3 -> x0, other arithmetic: 3.13 us -> none  [the longest x1 1.55 us: on_device(): dense[None].astype(F32)]
where the time goes in v2:
time: 108 us; the launch traced here: 107 us
  Pallas kernels  99.9 us (92%)
  local copies, waits for them, and re-layouts  6.31 us (6%)
    pallas_call x1, Pallas kernels, run_program(): pl.pallas_call(program_kernel, out_shape=[jax.ShapeDtypeStruct((4, rows,...  98.3 us
    unnamed x14, local copies, waits for them, and re-layouts  6.31 us

profile of v2, /device:TPU:0, one launch (start us, length us, event | category | flops | bytes accessed | tf_op | source)
XLA Modules:
  0.0 106.9 jit_solution(10829555371048728441)
XLA Ops:
  0.7 98.3 %layers.1 = (bf16[4,48,576]{2,1,0:T(8,128)(2,1)}, bf16[4,48,768]{2,1,0:T(8,128)(2,1)}, bf16[4,48,768]{2,1,0:T(8,128)(2,1)}, bf16[4,16,128]{2,1,0:T(8,128)(2,1)},...) custom-call(bf16[2,1,64,768]{3,2,1,0:T(8,128)(2,1)} %refs_0_.1, ...), custom_call_target="tpu_custom_call" | custom-call | tf_op jit(solution)/shard_map/layers/pallas_call | solution.py:653
  98.9 0.0 copy-start
  98.9 1.0 copy-done
  99.9 0.0 copy-start.1
  99.9 1.0 copy-done.1
  100.8 0.0 copy-start.2
  100.8 0.9 copy-done.2
  101.8 0.0 copy-start.3
  101.8 0.9 copy-done.3
  102.7 0.0 copy-start.4
  102.7 0.9 copy-done.4
  103.6 0.0 copy-start.5
  103.6 0.9 copy-done.5
  104.5 0.0 copy-start.6
  104.5 0.7 copy-done.6
  105.2 1.6 %lay_out.1 = (bf16[2,64,768]{2,1,0:T(8,128)(2,1)}, bf16[2,64,768]{2,1,0:T(8,128)(2,1)}, f32[1,48]{1,0:T(1,128)}, f32[1,48]{1,0:T(1,128)}, f32[1,48]{1,0:T(1,128)...) custom-call(bf16[4,48,576]{2,1,0:T(8,128)(2,1)S(1)} %copy-done.2, ...), custom_call_target="tpu_custom_call" | custom-call | tf_op jit(solution)/shard_map/lay_out/pallas_call | solution.py:760
Async XLA Ops:
  98.9 1.0 copy-start
  99.9 1.0 copy-start.1
  100.8 0.9 copy-start.2
  101.8 0.9 copy-start.3
  102.7 0.9 copy-start.4
  103.6 0.9 copy-start.5
  104.5 0.7 copy-start.6

commit v3 on v2

v3 whole, which is shorter than its diff:
```python
import math

import jax
import jax.numpy as jnp
import numpy as np
from jax import lax
from jax.experimental import pallas as pl
from jax.experimental.pallas import tpu as pltpu
from jax.sharding import PartitionSpec as P

MESH = pl.DeviceIdType.MESH
F32 = jnp.float32
BF16 = jnp.bfloat16
HD = 64
ROT = 16
WIDTH = 768
TOK = 64
HALF = 32
SPLIT = 128
LEN = 256
GROUP = 192
NEAR = (1, 3, 2)
PARTS = (0, 1)
MIB = 1024 * 1024

KINDS = ((48, 576, False), (48, 768, True), (48, 768, False), (16, 128, True))


def ring(value, by):
    return lax.rem(value + by, 4)


def places():
    owner = lax.axis_index("fsdp")
    return owner, lax.div(owner, 4), lax.rem(owner, 4)


def joined(u, v, x_first):
    return u * 4 + v if x_first else v * 4 + u


def remote(src, dst, send, recv, target):
    return pltpu.make_async_remote_copy(
        src_ref=src, dst_ref=dst, send_sem=send, recv_sem=recv, device_id=target, device_id_type=MESH
    )


def greet(targets):
    barrier = pltpu.get_barrier_semaphore()
    for target in targets:
        pl.semaphore_signal(barrier, inc=1, device_id=target, device_id_type=MESH)
    pl.semaphore_wait(barrier, len(targets))


def sheet_peers(x, z):
    return [{"fsdp": ring(x, d) * 4 + z} for d in (1, 2, 3)] + [
        {"fsdp": x * 4 + ring(z, d)} for d in (1, 2, 3)
    ]


def seq_peers(y):
    return [{"seq": ring(y, d)} for d in (1, 2, 3)]


def dot(a, b):
    return jnp.dot(a, b, preferred_element_type=F32)


def dot_nt(a, b):
    return lax.dot_general(a, b, (((1,), (1,)), ((), ())), preferred_element_type=F32)


def dot_tn(a, b):
    return lax.dot_general(a, b, (((0,), (0,)), ((), ())), preferred_element_type=F32)


def turn_tables(tab_ref, odd, sign):
    tables = []
    for i in range(3):
        table = jnp.where(odd, tab_ref[3 + i], tab_ref[i])
        if i and sign < 0:
            table = -table
        tables.append(jnp.concatenate([table] * 3, axis=1))
    return tables


def turn(values, tables):
    cosine, low_sine, high_sine = tables
    span = values.shape[1]
    return (
        values * cosine
        + pltpu.roll(values, span - 8, 1) * low_sine
        + pltpu.roll(values, 8, 1) * high_sine
    )


def pieces_of(h):
    chunks = [16 * t + 4 * h + i for t in range(3) for i in range(4)]
    return [(chunk // 3, chunk % 3) for chunk in chunks]


ORDER = (0, 3, 1, 2)
BACK = (2, 1, 4, 0, 3)


def program_kernel(*refs):
    (
        x_ref, cot_ref, pos_ref, tab_hbm, fg, fb, sg, sb, db, hb, qb, eb, q_hbm, e_hbm, s_hbm, d_hbm,
        out_q, out_e, out_s, out_v, out_d, lo_out, ig_out,
        tab_ref, qw, ew, qs, es, vs, vecf, wq, we, ws, wv, wd,
        dq, de, ds, dv, dd, hq, he, hs, hv, hd, aq, ae, as_, av, ad,
        fq, fe, fs, pq, pe, ps, mq, me, ms, mv, md, nq, ne, ns, nv, nd,
        xall, dyall, posall, part, psend, prec, qkvs, probs, ctx, acts, slopes,
        n1s, n2s, xhs, vrows, bqs, grows, staged, end_e, lsem,
        gsend, grecv, dsend, drecv, csend, crecv,
        asend, arecv, rsend, rrecv, posend, porecv,
        hsend, hrecv, wsend, wrecv, bsend, brecv, ysend, yrecv, osend, orecv,
    ) = refs
    micro = lax.axis_index("section")
    y = lax.axis_index("seq")
    owner, x, z = places()
    sibling = {"section": 1 - micro}
    holds = x == y

    def piece(i, a):
        return pl.ds(pl.multiple_of(a * SPLIT + i * HALF, HALF), HALF)

    peers = sheet_peers(x, z) + seq_peers(y) + [sibling]
    peers += [{"seq": ring(y, d), "section": 1 - micro} for d in (1, 2, 3)]
    barrier = pltpu.get_barrier_semaphore()
    for target in peers:
        pl.semaphore_signal(barrier, inc=1, device_id=target, device_id_type=MESH)

    def mine(rows):
        return pl.ds(pl.multiple_of(owner * rows, 16), rows)

    def band(l, i):
        return wd.at[l, pl.ds(pl.multiple_of(i * 48, 16), 48), :]

    shrink_rows = s_hbm.at[0, pl.ds(pl.multiple_of(48 * y, 16), 48), :]
    loads = [
        pltpu.make_async_copy(src, dst, lsem.at[i])
        for i, (src, dst) in enumerate(
            [(q_hbm.at[0], qw), (e_hbm.at[0], ew), (shrink_rows, ws.at[micro, mine(48), :])]
            + [(x_ref.at[micro, 0, HALF * a : HALF * (a + 1), :], xall.at[0, piece(y, a), :]) for a in PARTS]
            + [(cot_ref.at[micro, 0, HALF * a : HALF * (a + 1), :], dyall.at[1, piece(y, a), :]) for a in PARTS]
            + [(tab_hbm, tab_ref), (d_hbm.at[0], band(micro, z))]
        )
    ]
    for load in loads[:-1]:
        load.start()

    @pl.when(holds)
    def _():
        loads[-1].start()

    vecf[...] = jnp.zeros_like(vecf)
    for i, ref in enumerate((fg, fb, sg, sb, db, hb)):
        vecf[i : i + 1, 0:48] = ref[...].astype(F32)
    for k in range(3):
        vecf[7 + k : 8 + k, 0:48] = qb[:, 48 * k : 48 * k + 48].astype(F32)
    loads[0].wait()
    loads[1].wait()
    for h in range(4):

        @pl.when(y == h)
        def _():
            qs[...] = jnp.concatenate(
                [qw[:, WIDTH * t + GROUP * h : WIDTH * t + GROUP * (h + 1)] for t in range(3)], axis=1
            )
            es[...] = jnp.concatenate(
                [ew[:, GROUP * f + 48 * h : GROUP * f + 48 * h + 48] for f in range(16)], axis=1
            )
            vecf[6:7, 0:48] = eb[:, 48 * h : 48 * h + 48].astype(F32)

    vs[...] = vecf[...].astype(BF16)
    wholes = (wq, we, ws, wv, wd)

    def slot(t, l, s):
        rows = KINDS[t][0]
        return wholes[t].at[l, pl.ds(pl.multiple_of(s * rows, 16), rows), :]

    wq[micro, mine(48), :] = qs[...]
    we[micro, mine(48), :] = es[...]
    wv[micro, mine(16), :] = vs[...]
    shape = (TOK, TOK)
    level = lax.broadcasted_iota(jnp.int32, shape, 0) == lax.broadcasted_iota(jnp.int32, shape, 1)
    spots = jnp.where(level, jnp.broadcast_to(pos_ref[micro].astype(F32), shape), 0.0)
    spots = jnp.broadcast_to(jnp.sum(spots, axis=1, keepdims=True), (TOK, 128))
    for a in PARTS:
        posall[piece(y, a), :] = spots[HALF * a : HALF * (a + 1)]
    for load in loads[2:-1]:
        load.wait()

    @pl.when(holds)
    def _():
        loads[-1].wait()

    pl.semaphore_wait(barrier, len(peers))

    def axes(t, l):
        x_first = KINDS[t][2] ^ (l == 1)
        return (x, z, x_first) if x_first else (z, x, x_first)

    def gather_start(l):
        for t in ORDER:
            u, v, x_first = axes(t, l)
            for k, d in enumerate(NEAR):
                remote(
                    slot(t, l, owner), slot(t, l, owner), gsend.at[t, k], grecv.at[t, owner],
                    {"fsdp": joined(ring(u, d), v, x_first)},
                ).start()

        @pl.when(holds)
        def _():
            for k, d in enumerate(NEAR):
                remote(
                    band(l, z), band(l, z), dsend.at[k], drecv.at[z], {"fsdp": ring(x, d) * 4 + z}
                ).start()

    def gather_forward(l):
        for t, d in [(t, d) for d in (0, 1, 3, 2) for t in (0, 1)] + [(t, d) for t in (3, 2) for d in (0, 1, 3, 2)]:
            u, v, x_first = axes(t, l)
            s = joined(ring(u, 4 - d), v, x_first)
            if d:
                remote(slot(t, l, s), slot(t, l, s), gsend.at[t, 0], grecv.at[t, s], sibling).wait_recv()
            for k, e in enumerate(NEAR if t == 3 else (1, 3)):
                remote(
                    slot(t, l, s), slot(t, l, s), gsend.at[t, (3 + 3 * d if t == 3 else 3 + 2 * d) + k],
                    grecv.at[t, s], {"fsdp": joined(u, ring(v, e), x_first)},
                ).start()

        @pl.when(jnp.logical_not(holds))
        def _():
            remote(band(l, z), band(l, z), dsend.at[0], drecv.at[z], sibling).wait_recv()

        for k, e in enumerate(NEAR):
            remote(
                band(l, z), band(l, z), dsend.at[3 + k], drecv.at[z], {"fsdp": x * 4 + ring(z, e)}
            ).start()

    def gather_relay(l):
        for t in (0, 1, 2):
            u, v, x_first = axes(t, l)
            for w in (0, 2, 1, 3):
                back, ahead = (3, 1) if w < 2 else (1, 3)
                s = joined(w, ring(v, back), x_first)
                remote(slot(t, l, s), slot(t, l, s), gsend.at[t, 0], grecv.at[t, s], sibling).wait_recv()
                remote(
                    slot(t, l, s), slot(t, l, s), gsend.at[t, 11 + w], grecv.at[t, s],
                    {"fsdp": joined(u, ring(v, ahead), x_first)},
                ).start()

    def need(t, l):
        @pl.when(micro == l)
        def _():
            if t < 4:
                u, v, x_first = axes(t, l)
                for e, w in [(e, w) for e in NEAR for w in range(4)]:
                    if t == 3 or e == 2 or (w < 2) == (e == 3):
                        s = joined(w, ring(v, 4 - e), x_first)
                        remote(slot(t, l, s), slot(t, l, s), gsend.at[t, 0], grecv.at[t, s], sibling).wait_recv()
            else:
                for e in NEAR:
                    i = ring(z, 4 - e)
                    remote(band(l, i), band(l, i), dsend.at[0], drecv.at[i], sibling).wait_recv()
            remote(wholes[t].at[l], wholes[t].at[l], csend.at[t], crecv.at[t], sibling).start()

        @pl.when(micro != l)
        def _():
            remote(wholes[t].at[l], wholes[t].at[l], csend.at[t], crecv.at[t], sibling).wait_recv()

    def share(ref, a, sends, recvs):
        src = ref.at[piece(y, a), :]
        for k, d in enumerate(NEAR):
            remote(src, src, sends.at[a, k], recvs.at[a, k], {"seq": ring(y, d)}).start()

    def collect(ref, a, sends, recvs):
        for k, d in enumerate(NEAR):
            src = ref.at[piece(ring(y, 4 - d), a), :]
            remote(src, src, sends.at[a, k], recvs.at[a, k], sibling).wait_recv()

    def reduce_start(value, a, back, l):
        rows = slice(a * SPLIT, (a + 1) * SPLIT)
        part[back, l, rows] = value
        psend[back, l, rows] = value.astype(BF16)
        for k, d in enumerate(NEAR):
            to = ring(y, d)
            remote(
                psend.at[back, l, piece(to, a), :], prec.at[back, l, a, k],
                rsend.at[back, l, a, k], rrecv.at[back, l, a, k], {"seq": to},
            ).start()

    def reduce_end(a, back, l):
        total = part[back, l, piece(y, a), :]
        for k in range(3):
            remote(
                prec.at[back, l, a, k], prec.at[back, l, a, k],
                rsend.at[back, l, a, k], rrecv.at[back, l, a, k], sibling,
            ).wait_recv()
            total = total + prec[back, l, a, k].astype(F32)
        return total

    for a in PARTS:
        share(xall.at[0], a, asend.at[0, 0], arecv.at[0, 0])
        share(posall, a, posend, porecv)

    @pl.when(micro == 0)
    def _():
        gather_start(0)

    for a in PARTS:
        share(dyall.at[1], a, asend.at[1, 1], arecv.at[1, 1])

    @pl.when(micro == 0)
    def _():
        gather_forward(0)
        gather_relay(0)

    for a in PARTS:
        collect(posall, a, posend, porecv)

    def token_of(row):
        return (
            (lax.shift_right_logical(row, 5) & 3) * TOK + lax.shift_right_logical(row, 7) * HALF + (row & 31)
        )

    token = token_of(lax.broadcasted_iota(jnp.int32, (LEN, 128), 0))
    odd = posall[...] > (2 * token).astype(F32) + 0.5

    def forward(l):
        need(3, l)
        vrows[l] = jnp.concatenate(
            [wv[l, 16 * f : 16 * f + 16, 0:48].astype(F32) for f in range(16)], axis=1
        )
        for h in range(4):

            @pl.when(y == h)
            def _():
                bqs[l, 0:1, :] = jnp.concatenate(
                    [vrows[l, 7 + k : 8 + k, 48 * f : 48 * f + 48] for f, k in pieces_of(h)], axis=1
                )

        tables = turn_tables(tab_ref, odd, 1)
        for a in PARTS:
            rows = slice(a * SPLIT, (a + 1) * SPLIT)
            collect(xall.at[l], a, asend.at[0, l], arecv.at[0, l])
            values = xall[l, rows].astype(F32)
            center = values - jnp.mean(values, axis=-1, keepdims=True)
            scale = lax.rsqrt(jnp.mean(center * center, axis=-1, keepdims=True) + 1e-5)
            normed = center * scale
            xhs[l, rows] = normed
            n1 = (normed * vrows[l, 0:1, :] + vrows[l, 1:2, :]).astype(BF16)
            n1s[l, rows] = n1
            n2s[l, rows] = (normed * vrows[l, 2:3, :] + vrows[l, 3:4, :]).astype(BF16)
            if a == 0:
                need(0, l)
                if l == 0:

                    @pl.when(micro == 1)
                    def _():
                        gather_start(1)

            joint = dot(n1, wq[l]) + bqs[l, 0:1, :]
            turned = turn(joint[:, : 2 * GROUP], [table[rows] for table in tables])
            qkvs[l, rows, : 2 * GROUP] = turned.astype(BF16)
            qkvs[l, rows, 2 * GROUP :] = joint[:, 2 * GROUP :].astype(BF16)
        row = token_of(lax.broadcasted_iota(jnp.int32, (LEN, LEN), 0))
        allowed = row >= token_of(lax.broadcasted_iota(jnp.int32, (LEN, LEN), 1))
        for n in range(3):
            q = qkvs[l, :, n * HD : (n + 1) * HD]
            k = qkvs[l, :, GROUP + n * HD : GROUP + (n + 1) * HD]
            v = qkvs[l, :, 2 * GROUP + n * HD : 2 * GROUP + (n + 1) * HD]
            scores = jnp.where(allowed, dot_nt(q, k) * HD**-0.5, -1e30)
            powers = jnp.exp(scores - jnp.max(scores, axis=-1, keepdims=True))
            prob = powers / jnp.sum(powers, axis=-1, keepdims=True)
            probs[l, n] = prob
            ctx[l, :, n * HD : (n + 1) * HD] = dot(prob.astype(BF16), v).astype(BF16)
        if l == 0:

            @pl.when(micro == 1)
            def _():
                gather_forward(1)

        need(1, l)
        hidden = dot(n2s[l], we[l]) + vrows[l, 6:7, :]
        phi = 0.5 + 0.5 * lax.erf(hidden * math.sqrt(0.5))
        acts[l] = (hidden * phi).astype(BF16)
        need(4, l)
        need(2, l)
        for a in PARTS:
            rows = slice(a * SPLIT, (a + 1) * SPLIT)
            reduce_start(dot(ctx[l, rows], wd[l]) + dot(acts[l, rows], ws[l]), a, 0, l)
        density = jnp.exp(-0.5 * hidden * hidden) * (1.0 / math.sqrt(2.0 * math.pi))
        slopes[l] = phi + hidden * density

    def forward_end(a, l):
        total = reduce_end(a, 0, l)
        result = xall[l, piece(y, a), :].astype(F32) + total + vrows[l, 4:5, :] + vrows[l, 5:6, :]
        return result.astype(BF16)

    grads = (dq, de, ds, dv, dd)
    helds = (hq, he, hs, hv, hd)
    wides = (aq, ae, as_, av, ad)
    fars, passed = (fq, fe, fs), (pq, pe, ps)
    mids = (mq, me, ms, mv, md)
    narrows = (nq, ne, ns, nv, nd)
    outs = (out_q, out_e, out_s, out_v, out_d)

    def core_of(t, l):
        return 1 - l if t == 1 else l

    def on_core(todo, t, l):
        @pl.when(micro == core_of(t, l))
        def _():
            todo(t, l)

    def keep(t, l, value):
        rows = KINDS[t][0] if t < 4 else 48
        value = value.astype(BF16)
        for b in range(value.shape[0] // rows):
            piece = value[b * rows : (b + 1) * rows]
            if t < 4:
                grads[t][l, b // 4, b % 4] = piece
            else:
                grads[t][l, b] = piece

        @pl.when(micro != core_of(t, l))
        def _():
            remote(grads[t].at[l], helds[t], hsend.at[t], hrecv.at[t], sibling).start()

    def fold(t, l):
        remote(helds[t], helds[t], hsend.at[t], hrecv.at[t], sibling).wait_recv()
        grad, held = grads[t], helds[t]
        if t == 4:
            for i in range(4):
                grad[l, i] = (grad[l, i].astype(F32) + held[i].astype(F32)).astype(BF16)
            for k, e in enumerate(NEAR):
                to = ring(z, e)
                remote(
                    grad.at[l, to], wides[t].at[k], wsend.at[t, k], wrecv.at[t, k], {"fsdp": x * 4 + to}
                ).start()
            return

        def add(i, carry):
            a, b = lax.div(i, 4), lax.rem(i, 4)
            grad[l, a, b] = (grad[l, a, b].astype(F32) + held[a, b].astype(F32)).astype(BF16)
            return carry

        lax.fori_loop(0, 16, add, 0)
        u, v, x_first = axes(t, l)
        if t == 3:
            for k, e in enumerate(NEAR):
                to = ring(v, e)
                remote(
                    grad.at[l, :, to] if x_first else grad.at[l, to],
                    wides[t].at[k], wsend.at[t, k], wrecv.at[t, k], {"fsdp": joined(u, to, x_first)},
                ).start()
            return
        low, high = pl.ds(0, 2), pl.ds(2, 2)
        ahead, behind, across = ring(v, 1), ring(v, 3), ring(v, 2)
        for k, (half, to, dst, via) in enumerate(
            [
                (low, across, fars[t].at[0], ahead),
                (high, across, fars[t].at[1], behind),
                (high, ahead, wides[t].at[0, high], ahead),
                (low, behind, wides[t].at[1, low], behind),
            ]
        ):
            remote(
                grad.at[l, half, to] if x_first else grad.at[l, to, half],
                dst, wsend.at[t, k], wrecv.at[t, k], {"fsdp": joined(u, via, x_first)},
            ).start()

    def relay(t, l):
        grad = grads[t]
        u, v, x_first = axes(t, l)
        for i, to in enumerate((ring(v, 1), ring(v, 3))):
            remote(fars[t].at[i], fars[t].at[i], wsend.at[t, i], wrecv.at[t, i], sibling).wait_recv()
            for b in range(2):
                w = 2 * i + b
                near = grad[l, w, to] if x_first else grad[l, to, w]
                passed[t][i, b] = (near.astype(F32) + fars[t][i, b].astype(F32)).astype(BF16)
            remote(
                passed[t].at[i], wides[t].at[i, pl.ds(2 * i, 2)], wsend.at[t, 4 + i], wrecv.at[t, 4 + i],
                {"fsdp": joined(u, to, x_first)},
            ).start()

    def wide_end(t, l):
        grad = grads[t]
        terms = 3 if t > 2 else 2
        if t > 2:
            for k in range(3):
                remote(wides[t].at[k], wides[t].at[k], wsend.at[t, k], wrecv.at[t, k], sibling).wait_recv()
        else:
            for k, i in ((2, 0), (3, 1), (4, 0), (5, 1)):
                half = wides[t].at[i, pl.ds(0, 2)]
                remote(half, half, wsend.at[t, k], wrecv.at[t, k], sibling).wait_recv()
        if t == 4:
            total = grad[l, z].astype(F32)
            for k in range(3):
                total = total + wides[t][k].astype(F32)
            mids[t][...] = total.astype(BF16)

            @pl.when(jnp.logical_not(holds))
            def _():
                away = ring(x, 4 - y) - 1
                remote(
                    mids[t], narrows[t].at[away], bsend.at[t, 0], brecv.at[t, away], {"fsdp": y * 4 + z}
                ).start()

            return
        u, v, x_first = axes(t, l)
        for d in (1, 3, 2, 0):
            to = ring(u, d)
            total = grad[l, to, v].astype(F32) if x_first else grad[l, v, to].astype(F32)
            for k in range(terms):
                total = total + wides[t][k, to].astype(F32)
            mids[t][to] = total.astype(BF16)
            if d:
                k = NEAR.index(d)
                remote(
                    mids[t].at[to], narrows[t].at[k], bsend.at[t, k], brecv.at[t, k],
                    {"fsdp": joined(to, v, x_first)},
                ).start()

    def narrow_end(t, l):
        if t == 4:

            @pl.when(holds)
            def _():
                total = mids[t][...].astype(F32)
                for k in range(3):
                    remote(narrows[t].at[k], narrows[t].at[k], bsend.at[t, 0], brecv.at[t, k], sibling).wait_recv()
                    total = total + narrows[t][k].astype(F32)
                out_d[...] = total.astype(BF16)
                for k, d in enumerate(NEAR):
                    remote(out_d, out_d, ysend.at[t, k], yrecv.at[t, 0], {"seq": ring(y, d)}).start()

            return
        u, v, x_first = axes(t, l)
        total = mids[t][u].astype(F32)
        for k in range(3):
            remote(narrows[t].at[k], narrows[t].at[k], bsend.at[t, k], brecv.at[t, k], sibling).wait_recv()
            total = total + narrows[t][k].astype(F32)
        if t == 1:
            end_e[...] = total.astype(BF16)
            for k, d in enumerate(NEAR + (0,)):
                remote(
                    end_e, out_e.at[y], ysend.at[t, k], yrecv.at[t, k],
                    {"seq": ring(y, d), "section": 1 - micro},
                ).start()
            return
        outs[t][y] = total.astype(BF16)
        for k, d in enumerate(NEAR):
            remote(
                outs[t].at[y], outs[t].at[y], ysend.at[t, k], yrecv.at[t, k], {"seq": ring(y, d)}
            ).start()

    def arrive_back(l):
        pieces = []
        for a in PARTS:
            rows = slice(a * SPLIT, (a + 1) * SPLIT)
            collect(dyall.at[l], a, asend.at[1, l], arecv.at[1, l])
            out_grad = dyall[l, rows]
            pieces.append((dot_nt(out_grad, ws[l]) * slopes[l, rows]).astype(BF16))
        return jnp.concatenate(pieces, axis=0)

    def hidden_weights(l, hidden_grad):
        out_grad = dyall[l]
        keep(2, l, dot_tn(acts[l], out_grad))
        keep(1, l, dot_tn(n2s[l], hidden_grad))
        keep(4, l, dot_tn(ctx[l], out_grad))

    def attention_back(l):
        ctx_grad = dot_nt(dyall[l], wd[l]).astype(BF16)
        parts = ([], [], [])
        for n in range(3):
            q = qkvs[l, :, n * HD : (n + 1) * HD]
            k = qkvs[l, :, GROUP + n * HD : GROUP + (n + 1) * HD]
            v = qkvs[l, :, 2 * GROUP + n * HD : 2 * GROUP + (n + 1) * HD]
            up = ctx_grad[:, n * HD : (n + 1) * HD]
            prob = probs[l, n]
            prob_grad = dot_nt(up, v)
            inner = jnp.sum(prob * prob_grad, axis=-1, keepdims=True)
            score_grad = (prob * (prob_grad - inner)).astype(BF16)
            parts[0].append(dot(score_grad, k) * HD**-0.5)
            parts[1].append(dot_tn(score_grad, q) * HD**-0.5)
            parts[2].append(dot_tn(prob.astype(BF16), up))
        turned_grad = jnp.concatenate(parts[0] + parts[1], axis=1).astype(BF16).astype(F32)
        return jnp.concatenate(
            [turn(turned_grad, turn_tables(tab_ref, odd, -1))] + parts[2], axis=1
        ).astype(BF16)

    def vector_grads(l, hidden_grad, joint_grad, n1_grad, n2_grad):
        normed = xhs[l]
        grows[...] = jnp.zeros_like(grows)
        grows[0:1, :WIDTH] = jnp.sum(n1_grad * normed, axis=0, keepdims=True)
        grows[1:2, :WIDTH] = jnp.sum(n1_grad, axis=0, keepdims=True)
        grows[2:3, :WIDTH] = jnp.sum(n2_grad * normed, axis=0, keepdims=True)
        grows[3:4, :WIDTH] = jnp.sum(n2_grad, axis=0, keepdims=True)
        grows[4:5, :WIDTH] = sum(
            jnp.sum(dyall[l, piece(y, a), :].astype(F32), axis=0, keepdims=True) for a in PARTS
        )
        grows[6:7, :WIDTH] = jnp.sum(hidden_grad.astype(F32), axis=0, keepdims=True)
        joint_bias = jnp.sum(joint_grad.astype(F32), axis=0, keepdims=True)
        for h in range(4):

            @pl.when(y == h)
            def _():
                for i, (f, k) in enumerate(pieces_of(h)):
                    grows[7 + k : 8 + k, 48 * f : 48 * f + 48] = joint_bias[:, 48 * i : 48 * i + 48]

        keep(3, l, jnp.concatenate([grows[:, 48 * f : 48 * f + 128] for f in range(16)], axis=0))

    def backward_end(a, l):
        total = reduce_end(a, 1, l)
        values = xall[l, piece(y, a), :].astype(F32)
        center = values - jnp.mean(values, axis=-1, keepdims=True)
        scale = lax.rsqrt(jnp.mean(center * center, axis=-1, keepdims=True) + 1e-5)
        near = center * scale
        pulled = scale * (
            total
            - jnp.mean(total, axis=-1, keepdims=True)
            - near * jnp.mean(total * near, axis=-1, keepdims=True)
        )
        return (dyall[l, piece(y, a), :].astype(F32) + pulled).astype(BF16)

    def norm_back(l, hidden_grad, joint_grad):
        n1_grads, n2_grads = [], []
        for a in PARTS:
            rows = slice(a * SPLIT, (a + 1) * SPLIT)
            n1_grads.append(dot_nt(joint_grad[rows], wq[l]))
            n2_grads.append(dot_nt(hidden_grad[rows], we[l]))
            reduce_start(n1_grads[a] * vrows[l, 0:1, :] + n2_grads[a] * vrows[l, 2:3, :], a, 1, l)
        return jnp.concatenate(n1_grads, axis=0), jnp.concatenate(n2_grads, axis=0)

    forward(0)

    @pl.when(micro == 1)
    def _():
        gather_relay(1)

    for a in PARTS:
        middle = forward_end(a, 0)
        xall[1, piece(y, a), :] = middle
        share(xall.at[1], a, asend.at[0, 1], arecv.at[0, 1])
        staged[0, 0, HALF * a : HALF * (a + 1), :] = middle
    forward(1)

    hidden_grad = arrive_back(1)
    hidden_weights(1, hidden_grad)
    joint_grad = attention_back(1)
    n1_grad, n2_grad = norm_back(1, hidden_grad, joint_grad)
    keep(0, 1, dot_tn(n1s[1], joint_grad))
    for t in (2, 1, 4, 0):
        on_core(fold, t, 1)
    for a in PARTS:
        upper = backward_end(a, 1)
        dyall[0, piece(y, a), :] = upper
        share(dyall.at[0], a, asend.at[1, 0], arecv.at[1, 0])
        staged[1, 1, HALF * a : HALF * (a + 1), :] = upper
    vector_grads(1, hidden_grad, joint_grad, n1_grad, n2_grad)
    on_core(fold, 3, 1)
    for t in (2, 1, 0):
        on_core(relay, t, 1)
    for a in PARTS:
        staged[0, 1, HALF * a : HALF * (a + 1), :] = forward_end(a, 1)
    remote(staged.at[0, 1 - micro], lo_out.at[micro], osend.at[0], orecv.at[0], sibling).start()

    hidden_grad = arrive_back(0)
    hidden_weights(0, hidden_grad)
    joint_grad = attention_back(0)
    keep(0, 0, dot_tn(n1s[0], joint_grad))
    for t in (2, 1, 4):
        on_core(fold, t, 0)
    for t in BACK:
        on_core(wide_end, t, 1)
    n1_grad, n2_grad = norm_back(0, hidden_grad, joint_grad)
    on_core(fold, 0, 0)
    vector_grads(0, hidden_grad, joint_grad, n1_grad, n2_grad)
    on_core(fold, 3, 0)
    for t in BACK:
        on_core(narrow_end, t, 1)
    for t in (2, 1):
        on_core(relay, t, 0)
    for a in PARTS:
        staged[1, 0, HALF * a : HALF * (a + 1), :] = backward_end(a, 0)
    remote(staged.at[1, 1 - micro], ig_out.at[micro], osend.at[1], orecv.at[1], sibling).start()
    lo_out[micro] = staged[0, micro]
    ig_out[micro] = staged[1, micro]
    on_core(relay, 0, 0)
    for t in (4, 2, 1, 3, 0):
        on_core(wide_end, t, 0)
    for t in (4, 2, 1, 3, 0):
        on_core(narrow_end, t, 0)

    remote(end_e, out_e.at[y], ysend.at[1, 3], yrecv.at[1, 3], sibling).wait()
    for t in range(4):
        for k, d in enumerate(NEAR):
            src = outs[t].at[ring(y, 4 - d)]
            remote(src, src, ysend.at[t, k], yrecv.at[t, k], sibling).wait_recv()
            remote(src, src, ysend.at[t, k], yrecv.at[t, k], sibling).wait_send()
            remote(narrows[t].at[k], narrows[t].at[k], bsend.at[t, k], brecv.at[t, k], sibling).wait_send()
        for k in range(15):
            remote(slot(t, 0, 0), slot(t, 0, 0), gsend.at[t, k], grecv.at[t, 0], sibling).wait_send()
    for t in range(5):
        for k in range(6 if t < 3 else 3):
            src = wides[t].at[0, pl.ds(0, 2)] if t < 3 else wides[t].at[0]
            remote(src, src, wsend.at[t, k], wrecv.at[t, k], sibling).wait_send()
        remote(wholes[t].at[0], wholes[t].at[0], csend.at[t], crecv.at[t], sibling).wait_send()
        remote(helds[t], helds[t], hsend.at[t], hrecv.at[t], sibling).wait_send()

    @pl.when(holds)
    def _():
        for k in range(3):
            remote(out_d, out_d, ysend.at[4, k], yrecv.at[4, 0], sibling).wait_send()
            remote(band(0, 0), band(0, 0), dsend.at[k], drecv.at[0], sibling).wait_send()

    @pl.when(jnp.logical_not(holds))
    def _():
        remote(out_d, out_d, ysend.at[4, 0], yrecv.at[4, 0], sibling).wait_recv()
        remote(md, md, bsend.at[4, 0], brecv.at[4, 0], sibling).wait_send()

    for k in range(3):
        remote(band(0, 0), band(0, 0), dsend.at[3 + k], drecv.at[0], sibling).wait_send()
        for a in PARTS:
            src = posall.at[piece(y, a), :]
            remote(src, src, posend.at[a, k], porecv.at[a, k], sibling).wait_send()
            for l in range(2):
                for back in range(2):
                    src = xall.at[0, piece(y, a), :]
                    remote(src, src, asend.at[back, l, a, k], arecv.at[back, l, a, k], sibling).wait_send()
                    src = prec.at[back, l, a, k]
                    remote(src, src, rsend.at[back, l, a, k], rrecv.at[back, l, a, k], sibling).wait_send()
    for i, ref in enumerate((lo_out, ig_out)):
        remote(ref.at[0], ref.at[0], osend.at[i], orecv.at[i], sibling).wait()


def run_program(tokens, cot, positions, tables, vectors, weights):
    vmem = pl.BlockSpec(memory_space=pltpu.VMEM)
    hbm = pl.BlockSpec(memory_space=pl.ANY)
    dma = pltpu.SemaphoreType.DMA
    sizes = [(rows, cols) for rows, cols, _ in KINDS]

    def stacks(lead, dense_lead):
        return [pltpu.VMEM((*lead, rows, cols), BF16) for rows, cols in sizes] + [
            pltpu.VMEM((*dense_lead, 48, WIDTH), BF16)
        ]

    return pl.pallas_call(
        program_kernel,
        out_shape=[jax.ShapeDtypeStruct((4, rows, cols), BF16) for rows, cols in sizes]
        + [jax.ShapeDtypeStruct((48, WIDTH), BF16)]
        + [jax.ShapeDtypeStruct((2, TOK, WIDTH), BF16)] * 2,
        in_specs=[hbm, hbm, vmem, hbm] + [vmem] * 8 + [hbm] * 4,
        out_specs=[vmem] * 7,
        scratch_shapes=[
            pltpu.VMEM((6, LEN, 128), F32),
            pltpu.VMEM((48, 3 * WIDTH), BF16),
            pltpu.VMEM((48, 4 * WIDTH), BF16),
            pltpu.VMEM((48, 3 * GROUP), BF16),
            pltpu.VMEM((48, WIDTH), BF16),
            pltpu.VMEM((16, 128), BF16),
            pltpu.VMEM((16, 128), F32),
        ]
        + [pltpu.VMEM((2, 16 * rows, cols), BF16) for rows, cols in sizes]
        + [pltpu.VMEM((2, GROUP, WIDTH), BF16)]
        + stacks((2, 4, 4), (2, 4))
        + stacks((4, 4), (4,))
        + [pltpu.VMEM((2 if rows == 48 else 3, 4, rows, cols), BF16) for rows, cols in sizes]
        + [pltpu.VMEM((3, 48, WIDTH), BF16)]
        + [pltpu.VMEM((2, 2, rows, cols), BF16) for rows, cols in sizes[:3]] * 2
        + stacks((4,), ())
        + stacks((3,), (3,))
        + [
            pltpu.VMEM((2, LEN, WIDTH), BF16),
            pltpu.VMEM((2, LEN, WIDTH), BF16),
            pltpu.VMEM((LEN, 128), F32),
            pltpu.VMEM((2, 2, LEN, WIDTH), F32),
            pltpu.VMEM((2, 2, LEN, WIDTH), BF16),
            pltpu.VMEM((2, 2, 2, 3, HALF, WIDTH), BF16),
            pltpu.VMEM((2, LEN, 3 * GROUP), BF16),
            pltpu.VMEM((2, 3, LEN, LEN), F32),
            pltpu.VMEM((2, LEN, GROUP), BF16),
            pltpu.VMEM((2, LEN, WIDTH), BF16),
            pltpu.VMEM((2, LEN, WIDTH), F32),
            pltpu.VMEM((2, LEN, WIDTH), BF16),
            pltpu.VMEM((2, LEN, WIDTH), BF16),
            pltpu.VMEM((2, LEN, WIDTH), F32),
            pltpu.VMEM((2, 16, WIDTH), F32),
            pltpu.VMEM((2, 8, 3 * GROUP), F32),
            pltpu.VMEM((16, WIDTH + 128), F32),
            pltpu.VMEM((2, 2, TOK, WIDTH), BF16),
            pltpu.VMEM((48, WIDTH), BF16),
            dma((9,)),
            dma((4, 15)),
            dma((4, 16)),
            dma((6,)),
            dma((4,)),
            dma((5,)),
            dma((5,)),
            dma((2, 2, 2, 3)),
            dma((2, 2, 2, 3)),
            dma((2, 2, 2, 3)),
            dma((2, 2, 2, 3)),
            dma((2, 3)),
            dma((2, 3)),
            dma((5,)),
            dma((5,)),
            dma((5, 6)),
            dma((5, 6)),
            dma((5, 3)),
            dma((5, 3)),
            dma((5, 4)),
            dma((5, 4)),
            dma((2,)),
            dma((2,)),
        ],
        compiler_params=pltpu.CompilerParams(
            collective_id=1, has_side_effects=True, vmem_limit_bytes=58 * MIB
        ),
        name="layers",
    )(tokens, cot, positions, tables, *vectors, *weights)


def lay_out_kernel(
    q, e, s, v, d, lo, ig,
    lo_out, ig_out, o0, o1, o2, o3, q_out, qb_out, d_out, db_out, e_out, eb_out, s_out, sb_out,
):
    lo_out[...] = lo[...]
    ig_out[...] = ig[...]
    for t in range(3):
        for h in range(4):
            at = WIDTH * t + GROUP * h
            q_out[0, :, at : at + GROUP] = q[h, :, GROUP * t : GROUP * (t + 1)].astype(F32)
    for f in range(0, 16, 2):
        e_out[0, :, GROUP * f : GROUP * (f + 2)] = jnp.concatenate(
            [e[h, :, 48 * i : 48 * i + 48].astype(F32) for i in (f, f + 1) for h in range(4)], axis=1
        )
    for h in range(4):
        s_out[0, 48 * h : 48 * h + 48, :] = s[h].astype(F32)
    d_out[0] = d[...].astype(F32)
    total = v[0].astype(F32) + v[1].astype(F32) + v[2].astype(F32) + v[3].astype(F32)
    for i, ref in enumerate((o0, o1, o2, o3, db_out)):
        ref[...] = total[i : i + 1, 0:48]
    sb_out[...] = total[4:5, 0:48]
    qb_out[...] = jnp.concatenate([total[7 + k : 8 + k, 0:48] for k in range(3)], axis=1)
    eb_out[...] = jnp.concatenate([v[h].astype(F32)[6:7, 0:48] for h in range(4)], axis=1)


def lay_out(parts):
    vmem = pl.BlockSpec(memory_space=pltpu.VMEM)
    flat = jax.ShapeDtypeStruct((1, 48), F32)
    rows = jax.ShapeDtypeStruct((2, TOK, WIDTH), BF16)

    def wide(height, width):
        return jax.ShapeDtypeStruct((1, height, width), F32)

    shapes = [
        rows, rows, flat, flat, flat, flat, wide(48, 3 * WIDTH), jax.ShapeDtypeStruct((1, 144), F32),
        wide(48, WIDTH), flat, wide(48, 4 * WIDTH), jax.ShapeDtypeStruct((1, GROUP), F32),
        wide(GROUP, WIDTH), flat,
    ]
    return pl.pallas_call(
        lay_out_kernel,
        out_shape=shapes,
        in_specs=[vmem] * 7,
        out_specs=[vmem] * 14,
        compiler_params=pltpu.CompilerParams(vmem_limit_bytes=62 * MIB),
        name="lay_out",
    )(*parts)


def angle_tables():
    lane = np.arange(128) % HD
    frequency = np.exp(-math.log(10000.0) * (2.0 / ROT) * np.arange(ROT // 2)).astype(np.float32)
    tables = []
    for offset in (0, 1):
        row = np.arange(LEN)
        token = (row // HALF % 4) * TOK + row // SPLIT * HALF + row % HALF
        spots = (2 * token + offset).astype(np.float32)
        angle = (spots[:, None] * frequency[None, :])[:, lane % 8].astype(np.float64)
        cosine = np.where(lane < ROT, np.cos(angle), 1.0)
        low_sine = np.where(lane < 8, -np.sin(angle), 0.0)
        high_sine = np.where((lane >= 8) & (lane < ROT), np.sin(angle), 0.0)
        tables += [cosine, low_sine, high_sine]
    return np.stack(tables).astype(np.float32)


def on_device(
    tokens_in, cotangent, positions, first_gain, first_bias, second_gain, second_bias,
    qkv_weight, qkv_bias, dense_weight, dense_bias, expand_weight, expand_bias,
    shrink_weight, shrink_bias,
):
    parts = run_program(
        tokens_in,
        cotangent,
        positions,
        jnp.asarray(angle_tables()),
        (first_gain, first_bias, second_gain, second_bias, dense_bias, shrink_bias, qkv_bias, expand_bias),
        (qkv_weight, expand_weight, shrink_weight, dense_weight),
    )
    layer_out, input_grad, *rest = lay_out(parts)
    shape = (1, 2, 1, TOK, WIDTH)
    return (layer_out.reshape(shape), input_grad.reshape(shape), *rest)


def solution(mesh):
    tokens = P(None, "fsdp", "seq", None)
    flat = P("section", "fsdp")
    wide = P("section", "fsdp", None)
    out = P("section", None, "fsdp", "seq", None)
    return jax.shard_map(
        on_device,
        mesh=mesh,
        in_specs=(
            tokens, tokens, P(None, "fsdp", "seq"), flat, flat, flat, flat,
            wide, flat, wide, flat, wide, flat, wide, flat,
        ),
        out_specs=(
            out, out, flat, flat, flat, flat, wide, flat, wide, flat, wide, flat, wide, flat,
        ),
        check_vma=False,
    )
```

time: 108 us -> 103 us (0.954)
  local copies, waits for them, and re-layouts: 6.31 us -> 0 us
  Pallas kernels: 99.9 us -> 102 us
    unnamed x14 -> x0, local copies, waits for them, and re-layouts: 6.31 us -> none
    pallas_call x1, Pallas kernels: 1.63 us -> 3.01 us  [lay_out(): pl.pallas_call(lay_out_kernel, out_shape=shapes, in_specs=[vmem] * 7, out...]
where the time goes in v3:
time: 103 us
  Pallas kernels  102 us (99%)
    pallas_call x1, Pallas kernels, run_program(): pl.pallas_call(program_kernel, out_shape=[jax.ShapeDtypeStruct((4, rows,...  98.8 us
    pallas_call x1, Pallas kernels, lay_out(): pl.pallas_call(lay_out_kernel, out_shape=shapes, in_specs=[vmem] * 7, out...  3.01 us

profile of v3, /device:TPU:0, one launch (start us, length us, event | category | flops | bytes accessed | tf_op | source)
XLA Modules:
  0.0 102.5 jit_solution(683005111600633713)
XLA Ops:
  0.7 98.8 %layers.1 = (bf16[4,48,576]{2,1,0:T(8,128)(2,1)}, bf16[4,48,768]{2,1,0:T(8,128)(2,1)}, bf16[4,48,768]{2,1,0:T(8,128)(2,1)}, bf16[4,16,128]{2,1,0:T(8,128)(2,1)},...) custom-call(bf16[2,1,64,768]{3,2,1,0:T(8,128)(2,1)} %refs_0_.1, ...), custom_call_target="tpu_custom_call" | custom-call | tf_op jit(solution)/shard_map/layers/pallas_call | solution.py:751
  99.4 3.0 %lay_out.1 = (bf16[2,64,768]{2,1,0:T(8,128)(2,1)}, bf16[2,64,768]{2,1,0:T(8,128)(2,1)}, f32[1,48]{1,0:T(1,128)}, f32[1,48]{1,0:T(1,128)}, f32[1,48]{1,0:T(1,128)...) custom-call(bf16[4,48,576]{2,1,0:T(8,128)(2,1)} %get-tuple-element.3, ...), custom_call_target="tpu_custom_call" | custom-call | tf_op jit(solution)/shard_map/lay_out/pallas_call | solution.py:865

commit v4 on v3

--- a/solution.py
+++ b/solution.py
@@ -301,22 +301,21 @@
             total = total + prec[back, l, a, k].astype(F32)
         return total
 
+    @pl.when(micro == 0)
+    def _():
+        gather_start(0)
+
     for a in PARTS:
         share(xall.at[0], a, asend.at[0, 0], arecv.at[0, 0])
         share(posall, a, posend, porecv)
-
-    @pl.when(micro == 0)
-    def _():
-        gather_start(0)
-
-    for a in PARTS:
-        share(dyall.at[1], a, asend.at[1, 1], arecv.at[1, 1])
 
     @pl.when(micro == 0)
     def _():
         gather_forward(0)
         gather_relay(0)
 
+    for a in PARTS:
+        share(dyall.at[1], a, asend.at[1, 1], arecv.at[1, 1])
     for a in PARTS:
         collect(posall, a, posend, porecv)
 
@@ -672,24 +671,23 @@
     hidden_weights(0, hidden_grad)
     joint_grad = attention_back(0)
     keep(0, 0, dot_tn(n1s[0], joint_grad))
-    for t in (2, 1, 4):
+    for t in (2, 1, 0, 4):
         on_core(fold, t, 0)
     for t in BACK:
         on_core(wide_end, t, 1)
     n1_grad, n2_grad = norm_back(0, hidden_grad, joint_grad)
-    on_core(fold, 0, 0)
+    for t in (2, 1):
+        on_core(relay, t, 0)
     vector_grads(0, hidden_grad, joint_grad, n1_grad, n2_grad)
     on_core(fold, 3, 0)
     for t in BACK:
         on_core(narrow_end, t, 1)
-    for t in (2, 1):
-        on_core(relay, t, 0)
+    on_core(relay, 0, 0)
     for a in PARTS:
         staged[1, 0, HALF * a : HALF * (a + 1), :] = backward_end(a, 0)
     remote(staged.at[1, 1 - micro], ig_out.at[micro], osend.at[1], orecv.at[1], sibling).start()
     lo_out[micro] = staged[0, micro]
     ig_out[micro] = staged[1, micro]
-    on_core(relay, 0, 0)
     for t in (4, 2, 1, 3, 0):
         on_core(wide_end, t, 0)
     for t in (4, 2, 1, 3, 0):

time: 103 us -> 102 us (level)
  no operation moved by 1% of the time
where the time goes in v4:
time: 102 us
  Pallas kernels  101 us (99%)
    pallas_call x1, Pallas kernels, run_program(): pl.pallas_call(program_kernel, out_shape=[jax.ShapeDtypeStruct((4, rows,...  98 us
    pallas_call x1, Pallas kernels, lay_out(): pl.pallas_call(lay_out_kernel, out_shape=shapes, in_specs=[vmem] * 7, out...  3.01 us

profile of v4, /device:TPU:0, one launch (start us, length us, event | category | flops | bytes accessed | tf_op | source)
XLA Modules:
  0.0 101.7 jit_solution(8370055725648641806)
XLA Ops:
  0.7 98.0 %layers.1 = (bf16[4,48,576]{2,1,0:T(8,128)(2,1)}, bf16[4,48,768]{2,1,0:T(8,128)(2,1)}, bf16[4,48,768]{2,1,0:T(8,128)(2,1)}, bf16[4,16,128]{2,1,0:T(8,128)(2,1)},...) custom-call(bf16[2,1,64,768]{3,2,1,0:T(8,128)(2,1)} %refs_0_.1, ...), custom_call_target="tpu_custom_call" | custom-call | tf_op jit(solution)/shard_map/layers/pallas_call | solution.py:749
  98.7 3.0 %lay_out.1 = (bf16[2,64,768]{2,1,0:T(8,128)(2,1)}, bf16[2,64,768]{2,1,0:T(8,128)(2,1)}, f32[1,48]{1,0:T(1,128)}, f32[1,48]{1,0:T(1,128)}, f32[1,48]{1,0:T(1,128)...) custom-call(bf16[4,48,576]{2,1,0:T(8,128)(2,1)} %get-tuple-element.3, ...), custom_call_target="tpu_custom_call" | custom-call | tf_op jit(solution)/shard_map/lay_out/pallas_call | solution.py:863
